TPU v7x, 128 devices: a whole 4x4x4 slice. The times are simulated.
128 devices in a mesh: blk: 8 (over x, z_hi), grp: 16 (over z_lo, y, core).
Axes of the slice: x: 4, y: 4, z: 4 (z_hi: 2, z_lo: 2; z = z_hi * 2 + z_lo), core: 2. Of those that a mesh axis runs over, the one named last changes fastest.
Arguments:
- first_pooled_view: bfloat16 [16384, 4096], P(('blk', 'grp')), may hold values from -0.25 to 0.25
- second_pooled_view: bfloat16 [16384, 4096], P(('blk', 'grp')), may hold values from -0.25 to 0.25
- partner: int32 [128, 128], P(('blk', 'grp')), may hold values from 0 to 127, as said below
- adapter_down_weight: bfloat16 [4096, 64], replicated, may hold values from -0.09375 to 0.09375
- adapter_up_weight: bfloat16 [64, 1024], replicated, may hold values from -0.75 to 0.75
Outputs:
- loss: float32 [], replicated
- first_view_gradient: bfloat16 [16384, 4096], P(('blk', 'grp'))
- second_view_gradient: bfloat16 [16384, 4096], P(('blk', 'grp'))
- grad_down: float32 [4096, 64], replicated
- grad_up: float32 [64, 1024], replicated
Inputs may be any that keep to these rules, and one draw needn't show every extreme that they name: Each row of partner is a permutation of 0 to 127.
All inputs are finite; a program needn't handle non-finite values.
Results may differ from a plain program's by a relative error of at most 0.0076.
Values may be sent and summed in bfloat16 or wider, within the bound.
A program may use at most 192 MiB of HBM per device.

v0:
```python
import jax
import jax.numpy as jnp
from jax import lax
from jax.sharding import PartitionSpec as P

SCALE = 20.0
EPS = 1e-06


def from_behind(shard, axis, by):
    length = lax.axis_size(axis)
    return lax.ppermute(shard, axis, [(i, (i + by) % length) for i in range(length)])


def embed_texts(hidden_states, adapter_down_weight, adapter_up_weight):
    embedding_width = adapter_up_weight.shape[1]
    reduced_projection = jnp.dot(
        hidden_states, adapter_down_weight, preferred_element_type=jnp.float32
    ).astype(jnp.bfloat16)
    combined_states = hidden_states[:, :embedding_width].astype(jnp.float32) + jnp.dot(
        reduced_projection, adapter_up_weight, preferred_element_type=jnp.float32
    )
    inverse_norm = lax.rsqrt(
        jnp.sum(combined_states * combined_states, axis=1, keepdims=True) + EPS
    )
    return (reduced_projection, combined_states * inverse_norm, inverse_norm)


def adapter_backward(
    hidden_states,
    reduced_projection,
    normalized_rows,
    inverse_norm,
    normalized_gradient,
    adapter_down_weight,
    adapter_up_weight,
):
    grad_mixed = inverse_norm * (
        normalized_gradient
        - normalized_rows * jnp.sum(normalized_rows * normalized_gradient, axis=1, keepdims=True)
    )
    half_gradient = lax.optimization_barrier(grad_mixed.astype(jnp.bfloat16))
    reduced_gradient = jnp.dot(
        half_gradient, adapter_up_weight.T, preferred_element_type=jnp.float32
    ).astype(jnp.bfloat16)
    padded_states = jnp.pad(
        half_gradient.astype(jnp.float32),
        ((0, 0), (0, hidden_states.shape[1] - half_gradient.shape[1])),
    )
    state_gradient = (
        padded_states
        + jnp.dot(reduced_gradient, adapter_down_weight.T, preferred_element_type=jnp.float32)
    ).astype(jnp.bfloat16)
    down_term = lax.dot_general(
        hidden_states,
        reduced_gradient,
        (((0,), (0,)), ((), ())),
        preferred_element_type=jnp.float32,
    )
    up_term = lax.dot_general(
        reduced_projection,
        half_gradient,
        (((0,), (0,)), ((), ())),
        preferred_element_type=jnp.float32,
    )
    return (state_gradient, down_term, up_term)


def tile_exps(shared, current):
    scores = lax.dot_general(
        shared, current, (((1,), (1,)), ((), ())), preferred_element_type=jnp.float32
    )
    return jnp.exp(SCALE * scores - SCALE)


def shards(first_pooled_view, second_pooled_view, partner, adapter_down_weight, adapter_up_weight):
    row_count = first_pooled_view.shape[0]
    blocks = lax.axis_size("blk")
    blk_index = lax.axis_index("blk")
    grp_index = lax.axis_index("grp")
    text_count = row_count * blocks * lax.axis_size("grp")
    first_reduced, first_normalized, first_inverse_norm = embed_texts(
        first_pooled_view, adapter_down_weight, adapter_up_weight
    )
    second_reduced, second_normalized, second_inverse_norm = embed_texts(
        second_pooled_view, adapter_down_weight, adapter_up_weight
    )
    query_units = first_normalized.astype(jnp.bfloat16)
    key_units = second_normalized.astype(jnp.bfloat16)
    shared = lax.all_gather(query_units, "grp", axis=0, tiled=True)
    group_rows = shared.shape[0]
    emb_width = key_units.shape[1]
    row_sum = jnp.zeros((group_rows,), jnp.float32)
    current = key_units
    col_parts = []
    for step_index in range(blocks):
        if step_index > 0:
            current = from_behind(current, "blk", 1)
        exps_tile = tile_exps(shared, current)
        row_sum = row_sum + jnp.sum(exps_tile, axis=1)
        col_parts.append(jnp.sum(exps_tile, axis=0))
    row_total = lax.psum(row_sum, "grp")
    ordered = jnp.roll(jnp.stack(col_parts[::-1]), blk_index + 1, axis=0)
    col_all = lax.psum(ordered, "blk")
    col_own = lax.dynamic_index_in_dim(col_all, blk_index, 0, keepdims=False)
    row_own = lax.dynamic_slice_in_dim(row_total, grp_index * row_count, row_count)
    inv_rows = 1.0 / row_total
    query_part = jnp.zeros((group_rows, emb_width), jnp.float32)
    key_parts = []
    current = key_units
    for step_index in range(blocks):
        if step_index > 0:
            current = from_behind(current, "blk", 1)
        exps_tile = tile_exps(shared, current)
        col_here = lax.dynamic_index_in_dim(
            col_all, (blk_index + blocks - step_index) % blocks, 0, keepdims=False
        )
        weights = (0.5 * exps_tile * (inv_rows[:, None] + (1.0 / col_here)[None, :])).astype(
            jnp.bfloat16
        )
        query_part = query_part + jnp.dot(weights, current, preferred_element_type=jnp.float32)
        key_parts.append(
            lax.dot_general(
                weights, shared, (((0,), (0,)), ((), ())), preferred_element_type=jnp.float32
            )
        )
    query_own = lax.psum_scatter(query_part, "grp", scatter_dimension=0, tiled=True)
    stacked = jnp.roll(jnp.stack(key_parts[::-1]), blk_index + 1, axis=0)
    key_own = lax.psum_scatter(stacked, "blk", scatter_dimension=0, tiled=True)[0]
    pair_slots = partner[0]
    onehot = (pair_slots[:, None] == jnp.arange(row_count, dtype=jnp.int32)[None, :]).astype(
        jnp.bfloat16
    )
    pos_keys = jnp.dot(onehot, key_units, preferred_element_type=jnp.float32)
    pos_queries = lax.dot_general(
        onehot, query_units, (((0,), (0,)), ((), ())), preferred_element_type=jnp.float32
    )
    query_gradient = SCALE * (query_own - pos_keys)
    key_gradient = SCALE * (key_own - pos_queries)
    positive = SCALE * jnp.sum(query_units.astype(jnp.float32) * pos_keys)
    loss_part = 0.5 * jnp.sum(jnp.log(row_own)) + 0.5 * jnp.sum(jnp.log(col_own)) - positive
    first_view_gradient, first_down_product, first_up_product = adapter_backward(
        first_pooled_view,
        first_reduced,
        first_normalized,
        first_inverse_norm,
        query_gradient,
        adapter_down_weight,
        adapter_up_weight,
    )
    second_view_gradient, second_down_product, second_up_product = adapter_backward(
        second_pooled_view,
        second_reduced,
        second_normalized,
        second_inverse_norm,
        key_gradient,
        adapter_down_weight,
        adapter_up_weight,
    )
    loss_sum, grad_down, grad_up = lax.psum(
        (loss_part, first_down_product + second_down_product, first_up_product + second_up_product),
        ("blk", "grp"),
    )
    loss = loss_sum / text_count + SCALE
    return (loss, first_view_gradient, second_view_gradient, grad_down, grad_up)


def solution(mesh):
    in_specs = (P(("blk", "grp"), None), P(("blk", "grp"), None), P(("blk", "grp"), None), P(), P())
    out_specs = (P(), P(("blk", "grp"), None), P(("blk", "grp"), None), P(), P())
    return jax.shard_map(shards, mesh=mesh, in_specs=in_specs, out_specs=out_specs, check_vma=False)
```

profile of v0, /device:TPU:1, one launch (start us, length us, event | category | flops | bytes accessed | tf_op | source)
XLA Modules:
  0.0 506.1 jit_solution(3376270477884461356)
XLA Ops:
  8.2 1.7 convolution_convert_fusion.1
  9.9 1.4 multiply_reduce_fusion.4
  12.2 1.7 convolution_convert_fusion
  13.9 1.4 multiply_reduce_fusion.3
  16.2 4.5 collective-permute-start
  20.7 8.2 %collective-permute-done = bf16[128,1024]{1,0:T(8,128)(2,1)S(1)} collective-permute-done((bf16[128,1024]{1,0:T(8,128)(2,1)S(1)}, bf16[128,1024]{1,0:T(8,128)(2,1)S(1)}, u32[]{:S(2)}, u32[]{:S(2)}) %collective-permute-start) | collective-permute-done | bytes 262176 | tf_op jit(solution)/shard_map/ppermute | solution.py:12
  28.9 1.4 collective-permute-start.1
  30.3 10.3 %collective-permute-done.1 = bf16[128,1024]{1,0:T(8,128)(2,1)S(1)} collective-permute-done((bf16[128,1024]{1,0:T(8,128)(2,1)S(1)}, bf16[128,1024]{1,0:T(8,128)(2,1)S(1)}, u32[]{:S(2)}, u32[]{:S(2)}) %collective-permute-start.1) | collective-permute-done | bytes 262176 | tf_op jit(solution)/shard_map/ppermute | solution.py:12
  40.5 3.7 collective-permute-start.2
  44.2 10.4 %collective-permute-done.2 = bf16[128,1024]{1,0:T(8,128)(2,1)S(1)} collective-permute-done((bf16[128,1024]{1,0:T(8,128)(2,1)S(1)}, bf16[128,1024]{1,0:T(8,128)(2,1)S(1)}, u32[]{:S(2)}, u32[]{:S(2)}) %collective-permute-start.2) | collective-permute-done | bytes 262176 | tf_op jit(solution)/shard_map/ppermute | solution.py:12
  54.7 3.7 collective-permute-start.3
  58.4 5.4 %collective-permute-done.3 = bf16[128,1024]{1,0:T(8,128)(2,1)S(1)} collective-permute-done((bf16[128,1024]{1,0:T(8,128)(2,1)S(1)}, bf16[128,1024]{1,0:T(8,128)(2,1)S(1)}, u32[]{:S(2)}, u32[]{:S(2)}) %collective-permute-start.3) | collective-permute-done | bytes 262176 | tf_op jit(solution)/shard_map/ppermute | solution.py:12
  63.7 1.4 collective-permute-start.4
  65.1 7.4 %collective-permute-done.4 = bf16[128,1024]{1,0:T(8,128)(2,1)S(1)} collective-permute-done((bf16[128,1024]{1,0:T(8,128)(2,1)S(1)}, bf16[128,1024]{1,0:T(8,128)(2,1)S(1)}, u32[]{:S(2)}, u32[]{:S(2)}) %collective-permute-start.4) | collective-permute-done | bytes 262176 | tf_op jit(solution)/shard_map/ppermute | solution.py:12
  72.7 8.8 %collective-permute-done.5 = bf16[128,1024]{1,0:T(8,128)(2,1)} collective-permute-done((bf16[128,1024]{1,0:T(8,128)(2,1)S(1)}, bf16[128,1024]{1,0:T(8,128)(2,1)}, u32[]{:S(2)}, u32[]{:S(2)}) %collective-permute-start.5) | collective-permute-done | bytes 262176 | tf_op jit(solution)/shard_map/ppermute | solution.py:12
  81.6 3.7 fusion.54
  85.3 4.8 fusion.53
  90.1 2.3 fusion.52
  92.4 2.2 fusion.51
  94.6 2.3 fusion.50
  96.9 2.3 fusion.49
  99.2 2.3 fusion.48
  101.5 3.2 fusion.55
  104.8 20.5 %psum.36 = f32[8,128]{1,0:T(8,128)S(1)} all-reduce(f32[8,128]{1,0:T(8,128)S(1)} %constant_dynamic-slice_fusion.10), channel_id=1, replica_groups=mesh['blk'=8,'grp'=16] {'blk'}, use_global_device_ids=true, to_apply=%region_20.21 | all-reduce | flops 1024 | bytes 8192 | tf_op jit(solution)/shard_map/psum | solution.py:104
  125.3 38.5 %psum.35 = f32[2048]{0:T(1024)S(1)} all-reduce(f32[2048]{0:T(1024)S(1)} %add_add_fusion.1), channel_id=1, replica_groups=mesh['blk'=8,'grp'=16] {'grp'}, use_global_device_ids=true, to_apply=%region_10.0 | all-reduce | flops 2048 | bytes 16384 | tf_op jit(solution)/shard_map/psum | solution.py:102
  164.5 4.1 constant_dynamic-update-slice_fusion.15
  168.6 3.5 constant_dynamic-update-slice_fusion.14
  172.1 2.6 constant_dynamic-update-slice_fusion.13
  181.5 2.4 constant_dynamic-slice_fusion
  184.2 2.6 fusion.41
  186.9 4.5 fusion.44
  191.4 4.5 fusion.43
  196.0 4.5 fusion.42
  200.5 4.5 fusion.45
  205.0 4.5 fusion.46
  209.5 5.4 %fusion.47 = f32[2048,1024]{1,0:T(8,128)} fusion(bf16[128,1024]{1,0:T(8,128)(2,1)} %collective-permute-done.5, f32[2048,128]{1,0:T(8,128)S(1)} %copy-done.6, f32[128]{0:T(128)S(1)} %get-tuple-element.26, f32[2048]{0:T(1024)S(1)} %broadcast_divide_fusion), kind=kOutput, calls=%fused_computation.126 | convolution fusion | flops 537919488 | bytes 9708032 | tf_op jit(solution)/shard_map/dot_general | solution.py:121
  215.0 21.6 %add_add_fusion = f32[2048,1024]{1,0:T(8,128)} fusion(f32[2048,1024]{1,0:T(8,128)} %fusion.47, f32[2048,1024]{1,0:T(8,128)} %fusion.46, f32[2048,1024]{1,0:T(8,128)} %fusion.45, f32[2048,1024]{1,0:T(8,128)} %fusion.44, f32[2048,1024]{1,0:T(8,128)} %fusion.43, f32[2048,1024]{1,0:T(8,128)S(1)} %fusion.41, f32[2048,1024]{1,0:T(8,128)} %fusion.42, ...), kind=kOutput, calls=%fused_computation | convolution fusion | flops 552599552 | bytes 68428288 | tf_op jit(solution)/shard_map/dot_general | solution.py:121
  236.7 26.4 %reduce-scatter.5.cloned.1.call-done = f32[1,128,1024]{2,1,0:T(8,128)} async-done(((f32[8,128,1024]{2,1,0:T(8,128)}), f32[1,128,1024]{2,1,0:T(8,128)}) %reduce-scatter.5.cloned.1.call-update) | async-done | bytes 524304 | tf_op jit(solution)/shard_map/reduce_scatter | solution.py:129
  263.0 1.5 multiply_reduce_fusion
  264.9 71.3 %reduce-scatter.3.cloned.1.call-done = f32[128,1024]{1,0:T(8,128)} async-done(((f32[2048,1024]{1,0:T(8,128)}), f32[128,1024]{1,0:T(8,128)}) %reduce-scatter.3.cloned.1.call-update) | async-done | bytes 524304 | tf_op jit(solution)/shard_map/reduce_scatter | solution.py:127
  336.3 2.1 multiply_reduce_fusion.1
  340.9 1.5 fusion.56
  346.3 1.4 fusion.1
  347.8 68.4 %psum.37 = f32[]{:T(128)} all-reduce(f32[]{:T(128)S(6)} %sub.81), channel_id=1, replica_groups=mesh['blk'=8,'grp'=16] {'blk','grp'}, use_global_device_ids=true, to_apply=%region_23.24 | all-reduce | flops 1 | bytes 8 | tf_op jit(solution)/shard_map/psum | solution.py:160
  416.8 1.4 fusion
  418.3 76.3 %all-reduce.5.cloned.1.call-done = (f32[4096,64]{0,1:T(8,128)}, f32[64,1024]{1,0:T(8,128)}) async-done(((f32[4096,64]{0,1:T(8,128)}, f32[64,1024]{1,0:T(8,128)}), (f32[4096,64]{0,1:T(8,128)}, f32[64,1024]{1,0:T(8,128)})) %all-reduce.5.cloned.1.call-update) | async-done | bytes 1310736 | tf_op jit(solution)/shard_map/psum | solution.py:160
  494.5 2.3 copy.27
  496.8 1.7 copy.28
  (108 shorter events, 15.5 us)
Async XLA Ops:
  7.2 1.0 copy-start
  7.2 74.4 %all-gather.2.cloned.1.call-start = ((), (), s32[]{:S(2)}) async-start(), calls=%async_computation.2 | async-start | bytes 4456448 | tf_op jit(solution)/shard_map/all_gather | solution.py:90
  12.1 250.9 %reduce-scatter.5.cloned.1.call-start = ((), (), s32[]{:S(2)}) async-start(), calls=%async_computation.4 | async-start | bytes 4718592 | tf_op jit(solution)/shard_map/reduce_scatter | solution.py:129
  15.2 0.8 copy-start.3
  16.2 168.0 %copy-start.19 = (bf16[128,1024]{1,0:T(8,128)(2,1)}, bf16[128,1024]{1,0:T(8,128)(2,1)S(1)}, u32[]{:S(2)}) copy-start(bf16[128,1024]{1,0:T(8,128)(2,1)S(1)} %multiply_convert_fusion.10) | copy-start | bytes 786436
  16.2 12.7 %collective-permute-start = (bf16[128,1024]{1,0:T(8,128)(2,1)S(1)}, bf16[128,1024]{1,0:T(8,128)(2,1)S(1)}, u32[]{:S(2)}, u32[]{:S(2)}) collective-permute-start(bf16[128,1024]{1,0:T(8,128)(2,1)S(1)} %multiply_convert_fusion.10), channel_id=1, source_target_pairs={{0,16},{16,32},{32,48},{48,64},{64,80},{80,96},{96,112},{112,0},{1... | collective-permute-start | bytes 786440 | tf_op jit(solution)/shard_map/ppermute | solution.py:12
  28.9 68.1 %copy-start.21 = (bf16[128,1024]{1,0:T(8,128)(2,1)}, bf16[128,1024]{1,0:T(8,128)(2,1)S(1)}, u32[]{:S(2)}) copy-start(bf16[128,1024]{1,0:T(8,128)(2,1)S(1)} %collective-permute-done) | copy-start | bytes 786436
  28.9 11.6 %collective-permute-start.1 = (bf16[128,1024]{1,0:T(8,128)(2,1)S(1)}, bf16[128,1024]{1,0:T(8,128)(2,1)S(1)}, u32[]{:S(2)}, u32[]{:S(2)}) collective-permute-start(bf16[128,1024]{1,0:T(8,128)(2,1)S(1)} %collective-permute-done), channel_id=1, source_target_pairs={{0,16},{16,32},{32,48},{48,64},{64,80},{80,96},{96,112},{112,0},{1... | collective-permute-start | bytes 786440 | tf_op jit(solution)/shard_map/ppermute | solution.py:12
  40.5 54.1 %copy-start.23 = (bf16[128,1024]{1,0:T(8,128)(2,1)}, bf16[128,1024]{1,0:T(8,128)(2,1)S(1)}, u32[]{:S(2)}) copy-start(bf16[128,1024]{1,0:T(8,128)(2,1)S(1)} %collective-permute-done.1) | copy-start | bytes 786436
  40.5 14.2 %collective-permute-start.2 = (bf16[128,1024]{1,0:T(8,128)(2,1)S(1)}, bf16[128,1024]{1,0:T(8,128)(2,1)S(1)}, u32[]{:S(2)}, u32[]{:S(2)}) collective-permute-start(bf16[128,1024]{1,0:T(8,128)(2,1)S(1)} %collective-permute-done.1), channel_id=1, source_target_pairs={{0,16},{16,32},{32,48},{48,64},{64,80},{80,96},{96,112},{112,0},{1... | collective-permute-start | bytes 786440 | tf_op jit(solution)/shard_map/ppermute | solution.py:12
  54.7 17.9 %copy-start.29 = (bf16[128,1024]{1,0:T(8,128)(2,1)}, bf16[128,1024]{1,0:T(8,128)(2,1)S(1)}, u32[]{:S(2)}) copy-start(bf16[128,1024]{1,0:T(8,128)(2,1)S(1)} %collective-permute-done.2) | copy-start | bytes 786436
  54.7 9.1 %collective-permute-start.3 = (bf16[128,1024]{1,0:T(8,128)(2,1)S(1)}, bf16[128,1024]{1,0:T(8,128)(2,1)S(1)}, u32[]{:S(2)}, u32[]{:S(2)}) collective-permute-start(bf16[128,1024]{1,0:T(8,128)(2,1)S(1)} %collective-permute-done.2), channel_id=1, source_target_pairs={{0,16},{16,32},{32,48},{48,64},{64,80},{80,96},{96,112},{112,0},{1... | collective-permute-start | bytes 786440 | tf_op jit(solution)/shard_map/ppermute | solution.py:12
  63.7 26.4 %copy-start.25 = (bf16[128,1024]{1,0:T(8,128)(2,1)}, bf16[128,1024]{1,0:T(8,128)(2,1)S(1)}, u32[]{:S(2)}) copy-start(bf16[128,1024]{1,0:T(8,128)(2,1)S(1)} %collective-permute-done.3) | copy-start | bytes 786436
  63.7 8.8 %collective-permute-start.4 = (bf16[128,1024]{1,0:T(8,128)(2,1)S(1)}, bf16[128,1024]{1,0:T(8,128)(2,1)S(1)}, u32[]{:S(2)}, u32[]{:S(2)}) collective-permute-start(bf16[128,1024]{1,0:T(8,128)(2,1)S(1)} %collective-permute-done.3), channel_id=1, source_target_pairs={{0,16},{16,32},{32,48},{48,64},{64,80},{80,96},{96,112},{112,0},{1... | collective-permute-start | bytes 786440 | tf_op jit(solution)/shard_map/ppermute | solution.py:12
  72.6 9.0 %copy-start.27 = (bf16[128,1024]{1,0:T(8,128)(2,1)}, bf16[128,1024]{1,0:T(8,128)(2,1)S(1)}, u32[]{:S(2)}) copy-start(bf16[128,1024]{1,0:T(8,128)(2,1)S(1)} %collective-permute-done.4) | copy-start | bytes 786436
  72.6 8.9 %collective-permute-start.5 = (bf16[128,1024]{1,0:T(8,128)(2,1)S(1)}, bf16[128,1024]{1,0:T(8,128)(2,1)}, u32[]{:S(2)}, u32[]{:S(2)}) collective-permute-start(bf16[128,1024]{1,0:T(8,128)(2,1)S(1)} %collective-permute-done.4), channel_id=1, source_target_pairs={{0,16},{16,32},{32,48},{48,64},{64,80},{80,96},{96,112},{112,0},{1... | collective-permute-start | bytes 786440 | tf_op jit(solution)/shard_map/ppermute | solution.py:12
  81.5 20.0 %collective-permute-start.6 = (bf16[128,1024]{1,0:T(8,128)(2,1)}, bf16[128,1024]{1,0:T(8,128)(2,1)}, u32[]{:S(2)}, u32[]{:S(2)}) collective-permute-start(bf16[128,1024]{1,0:T(8,128)(2,1)} %collective-permute-done.5), channel_id=1, source_target_pairs={{0,16},{16,32},{32,48},{48,64},{64,80},{80,96},{96,112},{112,0},{1... | collective-permute-start | bytes 786440 | tf_op jit(solution)/shard_map/ppermute | solution.py:12
  81.6 8.6 %copy-start.1 = (bf16[2048,1024]{1,0:T(8,128)(2,1)S(1)}, bf16[2048,1024]{1,0:T(8,128)(2,1)}, u32[]{:S(2)}) copy-start(bf16[2048,1024]{1,0:T(8,128)(2,1)} %all-gather.2.cloned.1.call-done) | copy-start | bytes 12582916
  85.3 83.3 %copy-start.5 = (f32[2048,128]{1,0:T(8,128)}, f32[2048,128]{1,0:T(8,128)S(1)}, u32[]{:S(2)}) copy-start(f32[2048,128]{1,0:T(8,128)S(1)} %get-tuple-element.39) | copy-start | bytes 3145732
  85.3 7.1 %copy-start.30 = (bf16[128,1024]{1,0:T(8,128)(2,1)S(1)}, bf16[128,1024]{1,0:T(8,128)(2,1)}, u32[]{:S(2)}) copy-start(bf16[128,1024]{1,0:T(8,128)(2,1)} %copy-done.29) | copy-start | bytes 786436
  163.8 8.3 %copy-start.2 = (bf16[2048,1024]{1,0:T(8,128)(2,1)S(1)}, bf16[2048,1024]{1,0:T(8,128)(2,1)}, u32[]{:S(2)}) copy-start(bf16[2048,1024]{1,0:T(8,128)(2,1)} %all-gather.2.cloned.1.call-done) | copy-start | bytes 12582916
  164.5 10.3 %copy-start.8 = (f32[2048,128]{1,0:T(8,128)S(1)}, f32[2048,128]{1,0:T(8,128)}, u32[]{:S(2)}) copy-start(f32[2048,128]{1,0:T(8,128)} %get-tuple-element.41) | copy-start | bytes 3145732
  168.6 7.4 %copy-start.10 = (f32[2048,128]{1,0:T(8,128)S(1)}, f32[2048,128]{1,0:T(8,128)}, u32[]{:S(2)}) copy-start(f32[2048,128]{1,0:T(8,128)} %get-tuple-element.42) | copy-start | bytes 3145732
  172.1 5.2 %copy-start.12 = (f32[2048,128]{1,0:T(8,128)S(1)}, f32[2048,128]{1,0:T(8,128)}, u32[]{:S(2)}) copy-start(f32[2048,128]{1,0:T(8,128)} %get-tuple-element.43) | copy-start | bytes 3145732
  174.7 3.8 copy-start.14
  176.0 3.8 copy-start.16
  183.9 152.4 %reduce-scatter.3.cloned.1.call-start = ((), (), s32[]{:S(2)}) async-start(), calls=%async_computation.3 | async-start | bytes 8912896 | tf_op jit(solution)/shard_map/reduce_scatter | solution.py:127
  184.2 2.7 copy-start.11
  184.2 2.7 copy-start.31
  186.9 4.6 copy-start.13
  186.9 4.5 copy-start.24
  191.4 4.5 copy-start.15
  191.4 4.5 copy-start.22
  196.0 4.5 copy-start.9
  196.0 4.5 copy-start.26
  200.5 4.5 copy-start.7
  200.5 4.5 copy-start.28
  205.0 4.5 copy-start.6
  236.5 26.5 %copy-start.4 = (f32[128,1024]{1,0:T(8,128)S(1)}, f32[128,1024]{1,0:T(8,128)}, u32[]{:S(2)}) copy-start(f32[128,1024]{1,0:T(8,128)} %copy-done.3) | copy-start | bytes 1572868
  236.5 26.5 %copy-start.18 = (bf16[128,1024]{1,0:T(8,128)(2,1)S(1)}, bf16[128,1024]{1,0:T(8,128)(2,1)}, u32[]{:S(2)}) copy-start(bf16[128,1024]{1,0:T(8,128)(2,1)} %multiply_convert_fusion.11) | copy-start | bytes 786436
  236.5 26.5 %copy-start.32 = (s32[1,128]{1,0:T(1,128)S(1)}, s32[1,128]{1,0:T(1,128)}, u32[]{:S(2)}) copy-start(s32[1,128]{1,0:T(1,128)} %param.7) | copy-start | bytes 1540
  236.6 28.1 %copy-start.20 = (bf16[64,1024]{1,0:T(8,128)(2,1)S(1)}, bf16[64,1024]{1,0:T(8,128)(2,1)}, u32[]{:S(2)}) copy-start(bf16[64,1024]{1,0:T(8,128)(2,1)} %param.9) | copy-start | bytes 393220
  236.6 105.8 %copy-start.17 = (bf16[128,4096]{1,0:T(8,128)(2,1)S(1)}, bf16[128,4096]{1,0:T(8,128)(2,1)}, u32[]{:S(2)}) copy-start(bf16[128,4096]{1,0:T(8,128)(2,1)} %param.6) | copy-start | bytes 3145732
  236.6 257.9 %all-reduce.5.cloned.1.call-start = ((), (), s32[]{:S(2)}) async-start(), calls=%async_computation.5 | async-start | bytes 2621440 | tf_op jit(solution)/shard_map/psum | solution.py:160
Sparse Core Ops, SparseCore 0:
  12.2 48.2 all-gather.1
  184.0 78.9 reduce-scatter.4
  265.4 70.7 reduce-scatter.2
  343.8 150.6 all-reduce.4
where the time goes:
time: 507 us; the launch traced here: 506 us
  waiting for transfers between devices  225 us (44%)
  blocking collectives  127 us (25%)
  matrix products  109 us (21%)
  between operations  18.1 us (4%)
  starting transfers between devices  15.1 us (3%)
  local copies, waits for them, and re-layouts  8.61 us (2%)
    psum x1, waiting for transfers between devices, shards(): lax.psum((loss_part, first_down_product + second_down_product, first_up_p...  76.3 us
    reduce_scatter x1, waiting for transfers between devices, shards(): lax.psum_scatter(query_part, 'grp', scatter_dimension=0, tiled=True)  71.3 us
    psum x1, blocking collectives, shards(): lax.psum((loss_part, first_down_product + second_down_product, first_up_p...  68.4 us
    dot_general x8, matrix products, shards(): jnp.dot(weights, current, preferred_element_type=jnp.float32)  52.2 us
    ppermute x7, waiting for transfers between devices, from_behind(): lax.ppermute(shard, axis, [(i, (i + by) % length) for i in range(length)])  50.5 us
    psum x1, blocking collectives, shards(): row_total = lax.psum(row_sum, 'grp')  38.5 us
    reduce_scatter x1, waiting for transfers between devices, shards(): lax.psum_scatter(stacked, 'blk', scatter_dimension=0, tiled=True)[0]  26.4 us
    dot_general x8, matrix products, tile_exps(): lax.dot_general(shared, current, (((1,), (1,)), ((), ())), preferred_elem...  23.1 us
  transfers between devices with their start and end apart: 11, of which 9 were waited for; matrix products, arithmetic and copies ran while one was open for 16% of the time, Pallas kernels for 0%

commit v1 on v0

v1 whole, which is shorter than its diff:
```python
import jax
import jax.numpy as jnp
from jax import lax
from jax.experimental import pallas as pl
from jax.experimental.pallas import tpu as pltpu
from jax.sharding import PartitionSpec as P

SCALE = 20.0
EPS = 1e-06
MESH = pl.DeviceIdType.MESH
F32 = jnp.float32
BF16 = jnp.bfloat16

ROWS = 128
WIDTH = 1024
MODEL = 4096
RANK = 64
LANES = 128
TEXTS = 16384

OWN, UP, DOWN, PAIR, FAR, UP_PAIR, DOWN_PAIR, FAR_PAIR = range(8)
PLACE = {OWN: (0, 0), UP: (1, 0), DOWN: (3, 0), PAIR: (0, 1), FAR: (2, 0), UP_PAIR: (1, 1), DOWN_PAIR: (3, 1), FAR_PAIR: (2, 1)}
SLOT = {place: slot for slot, place in PLACE.items()}
HALF = ROWS // 2
COPIES = 160


def nn(a, b):
    return lax.dot_general(a, b, (((1,), (0,)), ((), ())), preferred_element_type=F32)


def nt(a, b):
    return lax.dot_general(a, b, (((1,), (1,)), ((), ())), preferred_element_type=F32)


def tn(a, b):
    return lax.dot_general(a, b, (((0,), (0,)), ((), ())), preferred_element_type=F32)


class Links:
    def __init__(self, send_sems, recv_sems):
        self.send_sems, self.recv_sems, self.count, self.sent = send_sems, recv_sems, 0, []

    def copy(self, src, dst, device):
        index = self.count
        self.count += 1
        made = pltpu.make_async_remote_copy(
            src_ref=src,
            dst_ref=dst,
            send_sem=self.send_sems.at[index],
            recv_sem=self.recv_sems.at[index],
            device_id=device,
            device_id_type=MESH,
        )
        made.start()
        self.sent.append(made)
        return made

    def settle(self, made):
        made.wait_recv()
        made.wait_send()
        self.sent = [copy for copy in self.sent if copy is not made]

    def drain(self):
        for made in self.sent:
            made.wait_send()
        self.sent = []


def body(
    h1_hbm, h2_hbm, partner_ref, down_hbm, up_ref,
    loss_ref, g1_ref, g2_ref, gdown_ref, gup_ref,
    h, down, unit, inv, low, q, k, expo, rowacc, colacc, rows, cols, row_in, row_pair_in, row_sib_in, col_in, col_pair_in,
    w, colb, pq, pk, sib_out, sib_in, q_out, q_in, k_out, k_in, pos, gm, gl,
    gsum, core_in, x_out, x_in, y_out, y_in, z_all, y_all, x_all, core_all,
    loss_core, loss_x, loss_y, loss_z,
    load_sems, send_sems, recv_sems,
):
    blk, grp = lax.axis_index("blk"), lax.axis_index("grp")
    x, z_hi = lax.div(blk, 2), lax.rem(blk, 2)
    z_lo, y, core = lax.div(grp, 8), lax.rem(lax.div(grp, 2), 4), lax.rem(grp, 2)
    z = z_hi * 2 + z_lo

    def at(dx=0, dy=0, dz=0, other=False):
        px, py, pz = lax.rem(x + dx, 4), lax.rem(y + dy, 4), lax.rem(z + dz, 4)
        pc = 1 - core if other else core
        return (px * 2 + lax.div(pz, 2), lax.rem(pz, 2) * 8 + py * 2 + pc)

    odd = lax.rem(z, 2)
    sibling = at(other=True)
    q_pair = at(dz=1 + 2 * odd)
    k_pair = at(dz=3 - 2 * odd)
    q_ring = {step: at(dy=step) for step in (1, 2, 3)}
    k_ring = {step: at(dx=step) for step in (1, 2, 3)}
    z_ring = {step: at(dz=step) for step in (1, 2, 3)}
    links = Links(send_sems, recv_sems)

    loads = [
        pltpu.make_async_copy(h1_hbm, h.at[0:ROWS], load_sems.at[0]),
        pltpu.make_async_copy(h2_hbm, h.at[ROWS : 2 * ROWS], load_sems.at[1]),
        pltpu.make_async_copy(down_hbm, down, load_sems.at[2]),
    ]
    for load in loads:
        load.start()
    barrier = pltpu.get_barrier_semaphore()
    partners = [sibling, *q_ring.values(), *k_ring.values(), *z_ring.values()]
    for device in partners:
        pl.semaphore_signal(barrier, inc=1, device_id=device, device_id_type=MESH)
    rowacc[...] = jnp.zeros_like(rowacc)
    colacc[...] = jnp.zeros_like(colacc)
    for load in loads:
        load.wait()

    reduced = nt(h[...], down[...]).astype(BF16)
    low[...] = reduced
    mixed = h[:, 0:WIDTH].astype(F32) + nn(reduced, up_ref[...])
    inverse = lax.rsqrt(jnp.sum(mixed * mixed, axis=1, keepdims=True) + EPS)
    inv[...] = jnp.broadcast_to(inverse, inv.shape)
    normal = mixed * inverse
    unit[...] = normal
    q[0:ROWS, :] = normal[0:ROWS].astype(BF16)
    k[0:ROWS, :] = normal[ROWS:].astype(BF16)
    pl.semaphore_wait(barrier, len(partners))

    def q_at(slot, half=None):
        first = slot * 2 * ROWS
        return q.at[first : first + ROWS] if half is None else q.at[first + half * HALF : first + (half + 1) * HALF]

    def k_at(slot, half=None):
        first = slot * ROWS
        return k.at[first : first + ROWS] if half is None else k.at[first + half * HALF : first + (half + 1) * HALF]

    def to_sibling(slot):
        first = slot * 2 * ROWS
        return links.copy(q.at[first : first + ROWS], q.at[first + ROWS : first + 2 * ROWS], sibling)

    first_hop = []
    for at_slot, ring, pair in ((q_at, q_ring, q_pair), (k_at, k_ring, k_pair)):
        first_hop.append(
            (
                links.copy(at_slot(OWN), at_slot(DOWN), ring[1]),
                links.copy(at_slot(OWN), at_slot(UP), ring[3]),
                links.copy(at_slot(OWN), at_slot(PAIR), pair),
            )
        )
    passed = {OWN: to_sibling(OWN)}
    second_hop = []
    for (from_down, from_up, _), (at_slot, ring) in zip(first_hop, ((q_at, q_ring), (k_at, k_ring))):
        from_down.wait_recv()
        one = links.copy(at_slot(DOWN, 0), at_slot(FAR, 0), ring[1])
        from_up.wait_recv()
        two = links.copy(at_slot(UP, 1), at_slot(FAR, 1), ring[3])
        second_hop.append((one, two))
    for slot in (DOWN, UP):
        passed[slot] = to_sibling(slot)
    pair_hop = []
    for (_, _, from_pair), (at_slot, ring) in zip(first_hop, ((q_at, q_ring), (k_at, k_ring))):
        from_pair.wait_recv()
        pair_hop.append(
            (
                links.copy(at_slot(PAIR), at_slot(DOWN_PAIR), ring[1]),
                links.copy(at_slot(PAIR), at_slot(UP_PAIR), ring[3]),
            )
        )
    passed[PAIR] = to_sibling(PAIR)

    def score(first_row, row_count, first_col, col_count):
        def chunk(step, carry):
            here = pl.ds(pl.multiple_of(first_row + step * 256, 256), 256)
            columns = pl.ds(first_col, col_count)
            value = jnp.exp(SCALE * nt(q[here, :], k[columns, :]) - SCALE)
            expo[here, columns] = value
            colacc[:, columns] += jnp.sum(value.reshape(32, 8, col_count), axis=0)
            total = value[:, 0:LANES]
            for lane in range(LANES, col_count, LANES):
                total = total + value[:, lane : lane + LANES]
            rowacc[here, :] += total
            return carry

        lax.fori_loop(0, row_count // 256, chunk, 0)

    for slot in (OWN, UP, DOWN, PAIR):
        passed[slot].wait_recv()
    score(0, 1024, 0, 512)
    third_hop = []
    for halves, (at_slot, pair) in zip(second_hop, ((q_at, q_pair), (k_at, k_pair))):
        for half in halves:
            half.wait_recv()
        third_hop.append(links.copy(at_slot(FAR), at_slot(FAR_PAIR), pair))
    passed[FAR] = to_sibling(FAR)
    for from_down, from_up in pair_hop:
        from_down.wait_recv()
        from_up.wait_recv()
    for slot in (DOWN_PAIR, UP_PAIR):
        passed[slot] = to_sibling(slot)
    score(0, 1024, 512, 256)
    for slot in (FAR, DOWN_PAIR, UP_PAIR):
        passed[slot].wait_recv()
    score(1024, 768, 0, 768)
    for arrival in third_hop:
        arrival.wait_recv()
    passed[FAR_PAIR] = to_sibling(FAR_PAIR)
    score(0, 1792, 768, 256)
    passed[FAR_PAIR].wait_recv()
    score(1792, 256, 0, 1024)
    links.drain()

    for block in range(16):
        lanes = rowacc[block * ROWS : (block + 1) * ROWS, :].T
        rows[block : block + 1, :] = jnp.sum(lanes, axis=0, keepdims=True)
    for block in range(8):
        cols[block : block + 1, :] = jnp.sum(colacc[:, block * LANES : (block + 1) * LANES], axis=0, keepdims=True)
    row_swap = links.copy(rows, row_sib_in, sibling)
    col_swap = {step: links.copy(cols, col_in.at[step - 1], k_ring[step]) for step in (1, 2, 3)}
    links.settle(row_swap)
    for slot in range(8):
        for rank in range(2):
            here, there = slot * 2 + rank, slot * 2 + 1 - rank
            rows[here : here + 1, :] = rows[here : here + 1, :] + row_sib_in[there : there + 1, :]
    row_copies = {step: links.copy(rows, row_in.at[step - 1], q_ring[step]) for step in (1, 2, 3)}

    def ring_sum(total, arrived, copies, width):
        for copy in copies.values():
            links.settle(copy)
        sums = []
        for slot in range(8):
            along, half = PLACE[slot]
            value = total[slot * width : (slot + 1) * width, :]
            for step in (1, 2, 3):
                there = SLOT[((along + step) % 4, half)]
                value = value + arrived[step - 1, there * width : (there + 1) * width, :]
            sums.append(value)
        for slot in range(8):
            total[slot * width : (slot + 1) * width, :] = sums[slot]

    def pair_sum(total, arrived, copy, width):
        links.settle(copy)
        for slot in range(8):
            along, half = PLACE[slot]
            there = SLOT[(along, 1 - half)]
            here = slice(slot * width, (slot + 1) * width)
            total[here, :] = total[here, :] + arrived[there * width : (there + 1) * width, :]

    ring_sum(cols, col_in, col_swap, 1)
    col_pair = links.copy(cols, col_pair_in, k_pair)
    ring_sum(rows, row_in, row_copies, 2)
    row_pair = links.copy(rows, row_pair_in, q_pair)
    pair_sum(cols, col_pair_in, col_pair, 1)
    col_half = 0.5 / cols[...]
    for block in range(8):
        colb[0:1, block * LANES : (block + 1) * LANES] = col_half[block : block + 1, :]
    pair_sum(rows, row_pair_in, row_pair, 2)

    choice = (lax.broadcasted_iota(jnp.int32, (ROWS, ROWS), 0) == partner_ref[...]).astype(BF16)
    pos[0:ROWS, :] = tn(choice, k[0:ROWS, :])
    pos[ROWS : 2 * ROWS, :] = nn(choice, q[0:ROWS, :])
    positive = SCALE * jnp.sum(q[0:ROWS, :].astype(F32) * pos[0:ROWS, :])
    terms = 0.5 * jnp.sum(jnp.log(rows[0:1, :])) + 0.5 * jnp.sum(jnp.log(cols[0:1, :])) - positive
    loss_core[core, :, :] = jnp.broadcast_to(terms, (8, LANES))
    loss_swap = [links.copy(loss_core.at[core], loss_core.at[core], sibling)]

    def loss_step(copies, before, after, place, ring):
        for copy in copies:
            copy.wait_recv()
        after[place, :, :] = jnp.sum(before[...], axis=0)
        return [links.copy(after.at[place], after.at[place], ring[step]) for step in (1, 2, 3)]

    row_half = 0.5 / rows[...]
    for block in range(16):
        rows[block : block + 1, :] = row_half[block : block + 1, :]

    def weigh(block, carry):
        here = pl.ds(pl.multiple_of(block * ROWS, ROWS), ROWS)
        row = jnp.broadcast_to(rows[pl.ds(block, 1), :], (ROWS, ROWS)).T
        for lane in range(0, WIDTH, LANES):
            columns = slice(lane, lane + LANES)
            w[here, columns] = (expo[here, columns] * (row + colb[0:1, columns])).astype(BF16)
        return carry

    lax.fori_loop(0, 16, weigh, 0)

    def key_part(first):
        pk[first : first + 256, :] = tn(w[:, first : first + 256], q[...])

    def query_part(slot):
        here = slot * 2 * ROWS
        part = nn(w[here : here + 2 * ROWS, :], k[...])
        pq[slot, :, :] = part[0:ROWS]
        sib_out[slot, :, :] = part[ROWS:].astype(BF16)
        return links.copy(sib_out.at[slot], sib_in.at[slot], sibling)

    def k_part(slot):
        return pk[slot * ROWS : (slot + 1) * ROWS, :]

    def q_part(slot):
        sib[slot].wait_recv()
        return pq[slot] + sib_in[slot].astype(F32)

    def send(value, out, landing, index, device):
        out[index, :, :] = value.astype(BF16)
        return links.copy(out.at[index], landing.at[index], device)

    k_got, q_got, sib = {}, {}, {}
    key_part(768)
    k_got[0] = send(k_part(FAR_PAIR), k_out, k_in, 0, k_pair)
    k_got[2] = send(k_part(DOWN_PAIR), k_out, k_in, 2, k_ring[3])
    for slot in (FAR_PAIR, DOWN_PAIR, UP_PAIR):
        sib[slot] = query_part(slot)
    key_part(512)
    k_got[1] = send(k_part(UP_PAIR), k_out, k_in, 1, k_ring[1])
    q_got[0] = send(q_part(FAR_PAIR), q_out, q_in, 0, q_pair)
    q_got[2] = send(q_part(DOWN_PAIR), q_out, q_in, 2, q_ring[3])
    q_got[1] = send(q_part(UP_PAIR), q_out, q_in, 1, q_ring[1])
    loss_copies = loss_step(loss_swap, loss_core, loss_x, x, k_ring)
    for slot in (FAR, PAIR, DOWN, UP, OWN):
        sib[slot] = query_part(slot)
    loss_copies = loss_step(loss_copies, loss_x, loss_y, y, q_ring)
    key_part(256)
    key_part(0)
    loss_copies = loss_step(loss_copies, loss_y, loss_z, z, z_ring)

    def far_halves(part, got, out, landing, ring):
        got[0].wait_recv()
        value = (part(FAR) + landing[0].astype(F32)).astype(BF16)
        out[3, :, :] = value
        return (
            links.copy(out.at[3, 0:HALF], landing.at[3, 0:HALF], ring[3]),
            links.copy(out.at[3, HALF:ROWS], landing.at[3, HALF:ROWS], ring[1]),
        )

    k_far = far_halves(k_part, k_got, k_out, k_in, k_ring)
    q_far = far_halves(q_part, q_got, q_out, q_in, q_ring)

    def pair_back(part, got, out, landing, pair):
        got[1].wait_recv()
        got[2].wait_recv()
        value = part(PAIR) + landing[1].astype(F32) + landing[2].astype(F32)
        got[6] = send(value, out, landing, 6, pair)

    pair_back(k_part, k_got, k_out, k_in, k_pair)
    pair_back(q_part, q_got, q_out, q_in, q_pair)

    def ring_back(part, got, far, out, landing, ring):
        far[0].wait_recv()
        value = part(DOWN)
        out[5, :, :] = jnp.concatenate([value[0:HALF] + landing[3, 0:HALF].astype(F32), value[HALF:]], axis=0).astype(BF16)
        got[5] = links.copy(out.at[5], landing.at[5], ring[3])
        far[1].wait_recv()
        value = part(UP)
        out[4, :, :] = jnp.concatenate([value[0:HALF], value[HALF:] + landing[3, HALF:ROWS].astype(F32)], axis=0).astype(BF16)
        got[4] = links.copy(out.at[4], landing.at[4], ring[1])

    ring_back(k_part, k_got, k_far, k_out, k_in, k_ring)
    ring_back(q_part, q_got, q_far, q_out, q_in, q_ring)
    for copy in loss_copies:
        copy.wait_recv()
    loss_ref[...] = jnp.sum(loss_z[...], axis=0) * (1.0 / TEXTS) + SCALE

    for view, (part, got, landing) in enumerate(((k_part, k_got, k_in), (q_part, q_got, q_in))):
        first = ROWS * (1 - view)
        here = slice(first, first + ROWS)
        for index in (4, 5, 6):
            got[index].wait_recv()
        total = part(OWN) + landing[4].astype(F32) + landing[5].astype(F32) + landing[6].astype(F32)
        gradient = SCALE * (total - pos[here, :])
        normal = unit[here, :]
        along = jnp.sum(normal * gradient, axis=1, keepdims=True)
        gm[here, :] = (inv[here, 0:1] * (gradient - normal * along)).astype(BF16)
    gl[...] = nt(gm[...], up_ref[...]).astype(BF16)
    low_rows = gl[...].astype(F32).T.astype(BF16)

    def down_chunk(step, carry):
        columns = pl.ds(pl.multiple_of(step * 512, 512), 512)
        gsum[:, columns] = nn(low_rows, h[:, columns])
        return carry

    lax.fori_loop(0, MODEL // 512, down_chunk, 0)
    gsum[:, MODEL : MODEL + WIDTH] = tn(low[...], gm[...])

    half_rows = RANK // 2
    quarter = (MODEL + WIDTH) // 4
    eighth = quarter // 2
    mine = pl.ds(pl.multiple_of(core * half_rows, half_rows), half_rows)
    theirs = pl.ds(pl.multiple_of((1 - core) * half_rows, half_rows), half_rows)
    core_all[...] = gsum[theirs, :].astype(BF16)
    core_got = links.copy(core_all, core_in, sibling)

    def state(first, out_ref, first_col, col_count, with_mixed):
        here = slice(first, first + ROWS)

        def chunk(step, carry):
            columns = pl.ds(pl.multiple_of(first_col + step * 512, 512), 512)
            value = nn(gl[here, :], down[:, columns])
            if with_mixed:
                value = value + gm[here, columns].astype(F32)
            out_ref[:, columns] = value.astype(BF16)
            return carry

        lax.fori_loop(0, col_count // 512, chunk, 0)

    core_got.wait_recv()
    for place in range(4):
        columns = slice(place * quarter, (place + 1) * quarter)
        value = gsum[mine, columns] + core_in[:, columns].astype(F32)
        gsum[mine, columns] = value
        x_out[place, :, :] = value.astype(BF16)
    x_got = {step: links.copy(x_out.at[lax.rem(x + step, 4)], x_in.at[step - 1], k_ring[step]) for step in (1, 2, 3)}
    state(0, g1_ref, 0, WIDTH, True)
    state(0, g1_ref, WIDTH, MODEL - WIDTH, False)
    for copy in x_got.values():
        copy.wait_recv()
    value = x_out[x].astype(F32) + x_in[0].astype(F32) + x_in[1].astype(F32) + x_in[2].astype(F32)
    for place in range(4):
        top, side = (place // 2) * 16, (place % 2) * eighth
        y_out[place, :, :] = value[top : top + 16, side : side + eighth].astype(BF16)
    y_got = {step: links.copy(y_out.at[lax.rem(y + step, 4)], y_in.at[step - 1], q_ring[step]) for step in (1, 2, 3)}
    state(ROWS, g2_ref, 0, WIDTH, True)
    for copy in y_got.values():
        copy.wait_recv()
    value = y_out[y].astype(F32) + y_in[0].astype(F32) + y_in[1].astype(F32) + y_in[2].astype(F32)
    z_all[z, :, :] = value.astype(BF16)
    z_got = [links.copy(z_all.at[z], z_all.at[z], z_ring[step]) for step in (1, 2, 3)]
    state(ROWS, g2_ref, WIDTH, MODEL - WIDTH, False)
    for copy in z_got:
        copy.wait_recv()
    y_all[y, :, :] = jnp.sum(z_all[...].astype(F32), axis=0).astype(BF16)
    y_back = [links.copy(y_all.at[y], y_all.at[y], q_ring[step]) for step in (1, 2, 3)]
    for copy in y_back:
        copy.wait_recv()
    for place in range(4):
        top, side = (place // 2) * 16, (place % 2) * eighth
        x_all[core, x, top : top + 16, side : side + eighth] = y_all[place]
    x_back = [links.copy(x_all.at[core, x], x_all.at[core, x], k_ring[step]) for step in (1, 2, 3)]
    core_sends = [links.copy(x_all.at[core, x], x_all.at[core, x], sibling)]
    for copy in x_back:
        copy.wait_recv()
    for step in (1, 2, 3):
        came = lax.rem(x + 4 - step, 4)
        core_sends.append(links.copy(x_all.at[core, came], x_all.at[core, came], sibling))
    for copy in core_sends:
        copy.wait_recv()
    for rank in range(2):
        top = slice(rank * half_rows, (rank + 1) * half_rows)
        for place in range(4):
            value = x_all[rank, place].astype(F32)
            first = place * quarter
            last = first + quarter
            if last <= MODEL:
                gdown_ref[top, first:last] = value
            else:
                gdown_ref[top, first:MODEL] = value[:, 0 : MODEL - first]
                gup_ref[top, :] = value[:, MODEL - first :]
    links.drain()


def shards(first_pooled_view, second_pooled_view, partner, adapter_down_weight, adapter_up_weight):
    vmem, hbm = pl.BlockSpec(memory_space=pltpu.VMEM), pl.BlockSpec(memory_space=pl.ANY)
    total = MODEL + WIDTH
    quarter = total // 4
    loss, first_gradient, second_gradient, down_rows, grad_up = pl.pallas_call(
        body,
        out_shape=(
            jax.ShapeDtypeStruct((8, LANES), F32),
            jax.ShapeDtypeStruct((ROWS, MODEL), BF16),
            jax.ShapeDtypeStruct((ROWS, MODEL), BF16),
            jax.ShapeDtypeStruct((RANK, MODEL), F32),
            jax.ShapeDtypeStruct((RANK, WIDTH), F32),
        ),
        in_specs=[hbm, hbm, vmem, hbm, vmem],
        out_specs=(vmem, vmem, vmem, vmem, vmem),
        scratch_shapes=[
            pltpu.VMEM((2 * ROWS, MODEL), BF16),
            pltpu.VMEM((RANK, MODEL), BF16),
            pltpu.VMEM((2 * ROWS, WIDTH), F32),
            pltpu.VMEM((2 * ROWS, LANES), F32),
            pltpu.VMEM((2 * ROWS, RANK), BF16),
            pltpu.VMEM((16 * ROWS, WIDTH), BF16),
            pltpu.VMEM((8 * ROWS, WIDTH), BF16),
            pltpu.VMEM((16 * ROWS, 8 * ROWS), F32),
            pltpu.VMEM((16 * ROWS, LANES), F32),
            pltpu.VMEM((8, 8 * ROWS), F32),
            pltpu.VMEM((16, LANES), F32),
            pltpu.VMEM((8, LANES), F32),
            pltpu.VMEM((3, 16, LANES), F32),
            pltpu.VMEM((16, LANES), F32),
            pltpu.VMEM((16, LANES), F32),
            pltpu.VMEM((3, 8, LANES), F32),
            pltpu.VMEM((8, LANES), F32),
            pltpu.VMEM((16 * ROWS, 8 * ROWS), BF16),
            pltpu.VMEM((8, 8 * ROWS), F32),
            pltpu.VMEM((8, ROWS, WIDTH), F32),
            pltpu.VMEM((8 * ROWS, WIDTH), F32),
            pltpu.VMEM((8, ROWS, WIDTH), BF16),
            pltpu.VMEM((8, ROWS, WIDTH), BF16),
            pltpu.VMEM((7, ROWS, WIDTH), BF16),
            pltpu.VMEM((7, ROWS, WIDTH), BF16),
            pltpu.VMEM((7, ROWS, WIDTH), BF16),
            pltpu.VMEM((7, ROWS, WIDTH), BF16),
            pltpu.VMEM((2 * ROWS, WIDTH), F32),
            pltpu.VMEM((2 * ROWS, WIDTH), BF16),
            pltpu.VMEM((2 * ROWS, RANK), BF16),
            pltpu.VMEM((RANK, total), F32),
            pltpu.VMEM((RANK // 2, total), BF16),
            pltpu.VMEM((4, RANK // 2, quarter), BF16),
            pltpu.VMEM((3, RANK // 2, quarter), BF16),
            pltpu.VMEM((4, 16, quarter // 2), BF16),
            pltpu.VMEM((3, 16, quarter // 2), BF16),
            pltpu.VMEM((4, 16, quarter // 2), BF16),
            pltpu.VMEM((4, 16, quarter // 2), BF16),
            pltpu.VMEM((2, 4, RANK // 2, quarter), BF16),
            pltpu.VMEM((RANK // 2, total), BF16),
            pltpu.VMEM((2, 8, LANES), F32),
            pltpu.VMEM((4, 8, LANES), F32),
            pltpu.VMEM((4, 8, LANES), F32),
            pltpu.VMEM((4, 8, LANES), F32),
            pltpu.SemaphoreType.DMA((3,)),
            pltpu.SemaphoreType.DMA((COPIES,)),
            pltpu.SemaphoreType.DMA((COPIES,)),
        ],
        compiler_params=pltpu.CompilerParams(
            collective_id=0, has_side_effects=True, vmem_limit_bytes=60 * 1024 * 1024
        ),
    )(first_pooled_view, second_pooled_view, partner, adapter_down_weight.T, adapter_up_weight)
    return (loss[0, 0], first_gradient, second_gradient, down_rows.T, grad_up)


def solution(mesh):
    in_specs = (P(("blk", "grp"), None), P(("blk", "grp"), None), P(("blk", "grp"), None), P(), P())
    out_specs = (P(), P(("blk", "grp"), None), P(("blk", "grp"), None), P(), P())
    return jax.shard_map(shards, mesh=mesh, in_specs=in_specs, out_specs=out_specs, check_vma=False)
```

time: 507 us -> 112 us (0.22)
  waiting for transfers between devices: 225 us -> 0 us
  blocking collectives: 127 us -> 0 us
  matrix products: 109 us -> 0 us
  Pallas kernels: 0 us -> 104 us
  between operations: 18.1 us -> 0.65 us
  starting transfers between devices: 15.1 us -> 0 us
    psum x3 -> x0, blocking collectives: 127 us -> none  [the longest x1 68.4 us: shards(): lax.psum((loss_part, first_down_product + second_down_product, first_up_p...]
    dot_general x38 -> x0, matrix products: 109 us -> none  [the longest x8 52.2 us: shards(): jnp.dot(weights, current, preferred_element_type=jnp.float32)]
    pallas_call x0 -> x1, Pallas kernels: none -> 104 us  [shards(): pl.pallas_call(body, out_shape=(jax.ShapeDtypeStruct((8, LANES), F32), ja...]
    reduce_scatter x2 -> x0, waiting for transfers between devices: 97.7 us -> none  [the longest x1 71.3 us: shards(): lax.psum_scatter(query_part, 'grp', scatter_dimension=0, tiled=True)]
    psum x1 -> x0, waiting for transfers between devices: 76.3 us -> none  [shards(): lax.psum((loss_part, first_down_product + second_down_product, first_up_p...]
    ppermute x7 -> x0, waiting for transfers between devices: 50.5 us -> none  [from_behind(): lax.ppermute(shard, axis, [(i, (i + by) % length) for i in range(length)])]
    ppermute x7 -> x0, starting transfers between devices: 14.7 us -> none  [from_behind(): lax.ppermute(shard, axis, [(i, (i + by) % length) for i in range(length)])]
  transfers between devices with their start and end apart: 11 -> 0, of which waited for: 9 -> 0; matrix products, arithmetic and copies ran while one was open for 16% -> 0% of each run, Pallas kernels for 0% -> 0%
where the time goes in v1:
time: 112 us; the launch traced here: 111 us
  Pallas kernels  104 us (93%)
  local copies, waits for them, and re-layouts  6.96 us (6%)
    pallas_call x1, Pallas kernels, shards(): pl.pallas_call(body, out_shape=(jax.ShapeDtypeStruct((8, LANES), F32), ja...  104 us
    unnamed x10, local copies, waits for them, and re-layouts  5.77 us

profile of v1, /device:TPU:1, one launch (start us, length us, event | category | flops | bytes accessed | tf_op | source)
XLA Modules:
  0.0 111.3 jit_solution(1124399448925175475)
XLA Ops:
  0.6 103.7 %shard_map.92 = (f32[8,128]{1,0:T(8,128)}, bf16[128,4096]{1,0:T(8,128)(2,1)}, bf16[128,4096]{1,0:T(8,128)(2,1)}, f32[64,4096]{1,0:T(8,128)}, f32[64,1024]{1,0:T(8,128)}) custom-call(bf16[128,4096]{1,0:T(8,128)(2,1)} %h1_hbm.1, bf16[128,4096]{1,0:T(8,128)(2,1)} %h2_hbm.1, s32[1,128]{1,0:T(1,128)} %partner_ref.1, bf16[64,4096]{1,0:T(8,128)(2,1)} %bitcast.4, ...), custom_call_target="tpu_custom_call" | custom-call | tf_op jit(solution)/shard_map/pallas_call | solution.py:460
  104.4 1.2 %slice.3 = f32[1,1]{1,0:T(1,128)} slice(f32[8,128]{1,0:T(8,128)} %get-tuple-element.10), slice={[0:1], [0:1]} | slice | bytes 8 | tf_op jit(solution)/shard_map/slice | solution.py:524
  105.6 0.0 copy-start.1
  105.6 2.4 %copy.14 = bf16[128,4096]{1,0:T(8,128)(2,1)} copy(bf16[128,4096]{1,0:T(8,128)(2,1)} %get-tuple-element.21) | data formatting | bytes 2097152
  107.9 0.0 copy-done.1
  107.9 0.0 copy-start
  107.9 1.0 copy.15
  108.9 0.6 copy-done
  109.5 0.0 copy-start.2
  109.5 1.0 copy.16
  110.5 0.1 copy-done.2
  110.6 0.7 copy.17
Async XLA Ops:
  105.6 2.4 %copy-start.1 = (bf16[128,4096]{1,0:T(8,128)(2,1)S(1)}, bf16[128,4096]{1,0:T(8,128)(2,1)}, u32[]{:S(2)}) copy-start(bf16[128,4096]{1,0:T(8,128)(2,1)} %get-tuple-element.22) | copy-start | bytes 3145732
  107.9 1.6 %copy-start = (f32[64,4096]{1,0:T(8,128)S(1)}, f32[64,4096]{1,0:T(8,128)}, u32[]{:S(2)}) copy-start(f32[64,4096]{1,0:T(8,128)} %get-tuple-element.13) | copy-start | bytes 3145732
  109.5 1.1 copy-start.2

commit v2 on v1

v2 whole, which is shorter than its diff:
```python
import jax
import jax.numpy as jnp
from jax import lax
from jax.experimental import pallas as pl
from jax.experimental.pallas import tpu as pltpu
from jax.sharding import PartitionSpec as P

SCALE = 20.0
EPS = 1e-06
MESH = pl.DeviceIdType.MESH
F32 = jnp.float32
BF16 = jnp.bfloat16

ROWS = 128
WIDTH = 1024
MODEL = 4096
RANK = 64
LANES = 128
TEXTS = 16384

ORDER = (0, 1, 2, 4, 3, 6, 5, 7)
SLOT = {mask: slot for slot, mask in enumerate(ORDER)}
BACK = {(7, 0): 1, (7, 1): 4}
BACK.update({(mask, half): link for mask, link in ((6, 2), (3, 1), (5, 4), (1, 1), (2, 2), (4, 4)) for half in (0, 1)})
HALF = ROWS // 2
COPIES = 176
TOTAL = MODEL + WIDTH
HALF_RANK = RANK // 2
PIECE = TOTAL // 8


def nn(a, b):
    return lax.dot_general(a, b, (((1,), (0,)), ((), ())), preferred_element_type=F32)


def nt(a, b):
    return lax.dot_general(a, b, (((1,), (1,)), ((), ())), preferred_element_type=F32)


def tn(a, b):
    return lax.dot_general(a, b, (((0,), (0,)), ((), ())), preferred_element_type=F32)


class Links:
    def __init__(self, send_sems, recv_sems):
        self.send_sems, self.recv_sems, self.count, self.sent = send_sems, recv_sems, 0, []

    def copy(self, src, dst, device):
        index = self.count
        self.count += 1
        made = pltpu.make_async_remote_copy(
            src_ref=src,
            dst_ref=dst,
            send_sem=self.send_sems.at[index],
            recv_sem=self.recv_sems.at[index],
            device_id=device,
            device_id_type=MESH,
        )
        made.start()
        self.sent.append(made)
        return made

    def settle(self, made):
        made.wait_recv()
        made.wait_send()
        self.sent = [copy for copy in self.sent if copy is not made]

    def drain(self):
        for made in self.sent:
            made.wait_send()
        self.sent = []


def half_rows(half):
    return slice(half * HALF, (half + 1) * HALF)


class Group:
    def __init__(self, links, near, data, stride, out, landing, part):
        self.links, self.near, self.data, self.stride = links, near, data, stride
        self.out, self.landing, self.part, self.got, self.back_got = out, landing, part, {}, {}

    def at(self, mask, half):
        first = SLOT[mask] * self.stride + half * HALF
        return self.data.at[first : first + HALF]

    def give(self, mask, half, link):
        there = mask ^ link
        self.got[there, half] = self.links.copy(self.at(mask, half), self.at(there, half), self.near[link])

    def have(self, mask, half):
        self.got[mask, half].wait_recv()

    def back(self, mask, half, add=None):
        rows = half_rows(half)
        value = self.part(mask, rows)
        if add is not None:
            self.back_got[add, half].wait_recv()
            value = value + self.landing[add - 1, rows].astype(F32)
        self.out[mask - 1, rows] = value.astype(BF16)
        self.back_got[mask, half] = self.links.copy(
            self.out.at[mask - 1, rows], self.landing.at[mask - 1, rows], self.near[BACK[mask, half]]
        )

    def whole(self):
        total = self.part(0, slice(0, ROWS))
        for mask in (1, 2, 4):
            for half in (0, 1):
                self.back_got[mask, half].wait_recv()
        for mask in (1, 2, 4):
            total = total + self.landing[mask - 1].astype(F32)
        return total


def body(
    h1_hbm, h2_hbm, partner_ref, down_hbm, up_ref,
    loss_ref, gl, gm, sums,
    h, down, unit, inv, low, q, k, expo, rowacc, colacc, rows, cols, row_in, row_sib_in, col_in,
    w, colb, pq, pk, sib_out, sib_in, q_out, q_in, k_out, k_in, pos,
    gsum, gsend, core_in, plane_out, plane_in, z_all,
    loss_core, loss_plane, loss_z,
    load_sems, send_sems, recv_sems,
):
    blk, grp = lax.axis_index("blk"), lax.axis_index("grp")
    x, z_hi = lax.div(blk, 2), lax.rem(blk, 2)
    z_lo, y, core = lax.div(grp, 8), lax.rem(lax.div(grp, 2), 4), lax.rem(grp, 2)
    z = z_hi * 2 + z_lo
    place = x * 4 + y

    def at(dx=0, dy=0, dz=0, other=False):
        px, py, pz = lax.rem(x + dx, 4), lax.rem(y + dy, 4), lax.rem(z + dz, 4)
        pc = 1 - core if other else core
        return (px * 2 + lax.div(pz, 2), lax.rem(pz, 2) * 8 + py * 2 + pc)

    up_or_down = [1 + 2 * lax.rem(c, 2) for c in (x, y, z)]

    def cube(flip):
        steps = [4 - s if flip else s for s in up_or_down]
        return {m: at(*(s if m & bit else 0 for bit, s in zip((1, 2, 4), steps))) for m in range(1, 8)}

    sibling = at(other=True)
    q_near, k_near = cube(False), cube(True)
    plane = {(dx, dy): at(dx, dy) for dx in range(4) for dy in range(4) if dx or dy}
    column = {dz: at(dz=dz) for dz in (1, 2, 3)}
    links = Links(send_sems, recv_sems)

    loads = [
        pltpu.make_async_copy(h1_hbm, h.at[0:ROWS], load_sems.at[0]),
        pltpu.make_async_copy(h2_hbm, h.at[ROWS : 2 * ROWS], load_sems.at[1]),
        pltpu.make_async_copy(down_hbm, down, load_sems.at[2]),
    ]
    for load in loads:
        load.start()
    partners = [sibling, *plane.values(), *column.values()]
    partners += [near[m] for near in (q_near, k_near) for m in (5, 6, 7)]
    barrier = pltpu.get_barrier_semaphore()
    for device in partners:
        pl.semaphore_signal(barrier, inc=1, device_id=device, device_id_type=MESH)
    rowacc[...] = jnp.zeros_like(rowacc)
    colacc[...] = jnp.zeros_like(colacc)
    for load in loads:
        load.wait()

    low[...] = nt(h[...], down[...]).astype(BF16)
    for view, own in enumerate((q, k)):
        here = slice(view * ROWS, (view + 1) * ROWS)
        mixed = h[here, 0:WIDTH].astype(F32) + nn(low[here, :], up_ref[...])
        inverse = lax.rsqrt(jnp.sum(mixed * mixed, axis=1, keepdims=True) + EPS)
        inv[here, :] = jnp.broadcast_to(inverse, (ROWS, LANES))
        normal = mixed * inverse
        unit[here, :] = normal
        own[0:ROWS, :] = normal.astype(BF16)
    pl.semaphore_wait(barrier, len(partners))

    sib = {}

    def q_part(mask, here):
        return pq[SLOT[mask], here, :] + sib_in[SLOT[mask], here, :].astype(F32)

    def k_part(mask, here):
        first = SLOT[mask] * ROWS
        return pk[first + here.start : first + here.stop, :]

    queries = Group(links, q_near, q, 2 * ROWS, q_out, q_in, q_part)
    keys = Group(links, k_near, k, ROWS, k_out, k_in, k_part)
    groups = (queries, keys)

    def to_sibling(mask):
        first = SLOT[mask] * 2 * ROWS
        return links.copy(q.at[first : first + ROWS], q.at[first + ROWS : first + 2 * ROWS], sibling)

    FIRST = {1: 0, 2: 1, 4: 0}
    NEXT = {4: 2, 2: 1, 1: 4}
    for turn in (0, 1):
        for group in groups:
            for link in (1, 2, 4):
                group.give(0, FIRST[link] ^ turn, link)
    passed = {0: to_sibling(0)}
    for turn in (0, 1):
        for group in groups:
            for mask in (4, 2, 1):
                group.have(mask, FIRST[mask] ^ turn)
                group.give(mask, FIRST[mask] ^ turn, NEXT[mask])
    for mask in (1, 2, 4):
        passed[mask] = to_sibling(mask)

    def score(first_row, row_count, first_col, col_count):
        def chunk(step, carry):
            here = pl.ds(pl.multiple_of(first_row + step * 256, 256), 256)
            columns = pl.ds(first_col, col_count)
            value = jnp.exp(SCALE * nt(q[here, :], k[columns, :]) - SCALE)
            expo[here, columns] = value
            colacc[:, columns] += jnp.sum(value.reshape(32, 8, col_count), axis=0)
            total = value[:, 0:LANES]
            for lane in range(LANES, col_count, LANES):
                total = total + value[:, lane : lane + LANES]
            rowacc[here, :] += total
            return carry

        lax.fori_loop(0, row_count // 256, chunk, 0)

    for mask in (0, 1, 2, 4):
        passed[mask].wait_recv()
    score(0, 1024, 0, 512)
    for group in groups:
        group.have(6, 0)
        group.give(6, 0, 1)
        group.have(3, 1)
        group.give(3, 1, 4)
    for mask, half in ((6, 1), (3, 0), (5, 0), (5, 1)):
        for group in groups:
            group.have(mask, half)
    for mask in (3, 6, 5):
        passed[mask] = to_sibling(mask)
    score(0, 1024, 512, 256)
    for mask in (3, 6, 5):
        passed[mask].wait_recv()
    score(1024, 768, 0, 768)
    for half in (0, 1):
        queries.have(7, half)
    passed[7] = to_sibling(7)
    for half in (0, 1):
        keys.have(7, half)
    score(0, 1792, 768, 256)
    passed[7].wait_recv()
    score(1792, 256, 0, 1024)
    links.drain()

    for block in range(8):
        cols[block : block + 1, :] = jnp.sum(colacc[:, block * LANES : (block + 1) * LANES], axis=0, keepdims=True)
    col_copies = {m: links.copy(cols, col_in.at[m - 1], k_near[m]) for m in range(1, 8)}
    for block in range(16):
        lanes = rowacc[block * ROWS : (block + 1) * ROWS, :].T
        rows[block : block + 1, :] = jnp.sum(lanes, axis=0, keepdims=True)
    row_swap = links.copy(rows, row_sib_in, sibling)
    links.settle(row_swap)
    for slot in range(8):
        for rank in range(2):
            here, there = slot * 2 + rank, slot * 2 + 1 - rank
            rows[here : here + 1, :] = rows[here : here + 1, :] + row_sib_in[there : there + 1, :]
    row_copies = {m: links.copy(rows, row_in.at[m - 1], q_near[m]) for m in range(1, 8)}

    choice = (lax.broadcasted_iota(jnp.int32, (ROWS, ROWS), 0) == partner_ref[...]).astype(BF16)
    pos[0:ROWS, :] = tn(choice, k[0:ROWS, :])
    pos[ROWS : 2 * ROWS, :] = nn(choice, q[0:ROWS, :])
    positive = SCALE * jnp.sum(q[0:ROWS, :].astype(F32) * pos[0:ROWS, :])

    def cube_sum(total, arrived, copies, width):
        for copy in copies.values():
            links.settle(copy)
        sums = []
        for mask in ORDER:
            value = total[SLOT[mask] * width : (SLOT[mask] + 1) * width, :]
            for m in range(1, 8):
                there = SLOT[mask ^ m] * width
                value = value + arrived[m - 1, there : there + width, :]
            sums.append(value)
        return sums

    sums_of_cols = cube_sum(cols, col_in, col_copies, 1)
    for slot, value in enumerate(sums_of_cols):
        colb[0:1, slot * LANES : (slot + 1) * LANES] = 0.5 / value
    sums_of_rows = cube_sum(rows, row_in, row_copies, 2)
    for slot, value in enumerate(sums_of_rows):
        rows[2 * slot : 2 * slot + 2, :] = 0.5 / value

    def weigh(block, carry):
        here = pl.ds(pl.multiple_of(block * ROWS, ROWS), ROWS)
        row = jnp.broadcast_to(rows[pl.ds(block, 1), :], (ROWS, ROWS)).T
        for lane in range(0, WIDTH, LANES):
            columns = slice(lane, lane + LANES)
            w[here, columns] = (expo[here, columns] * (row + colb[0:1, columns])).astype(BF16)
        return carry

    lax.fori_loop(0, 16, weigh, 0)

    def key_part(first):
        pk[first : first + 256, :] = tn(w[:, first : first + 256], q[...])

    def query_part(mask):
        slot = SLOT[mask]
        here = slot * 2 * ROWS
        part = nn(w[here : here + 2 * ROWS, :], k[...])
        pq[slot, :, :] = part[0:ROWS]
        sib_out[slot, :, :] = part[ROWS:].astype(BF16)
        sib[mask] = links.copy(sib_out.at[slot], sib_in.at[slot], sibling)

    key_part(768)
    for mask, half in ((7, 0), (7, 1), (5, 0), (5, 1)):
        keys.back(mask, half)
    query_part(7)
    key_part(512)
    keys.back(3, 0)
    keys.back(6, 1)
    sib[7].wait_recv()
    queries.back(7, 0)
    queries.back(7, 1)
    for mask in (5, 3, 6):
        query_part(mask)
    sib[5].wait_recv()
    queries.back(5, 0)
    queries.back(5, 1)
    sib[3].wait_recv()
    queries.back(3, 0)
    sib[6].wait_recv()
    queries.back(6, 1)

    terms = 0.5 * jnp.sum(jnp.log(sums_of_rows[0][0:1, :])) + 0.5 * jnp.sum(jnp.log(sums_of_cols[0])) - positive
    loss_core[core, :, :] = jnp.broadcast_to(terms, (8, LANES))
    loss_swap = links.copy(loss_core.at[core], loss_core.at[core], sibling)
    key_part(256)
    keys.back(6, 0, 7)
    keys.back(3, 1, 7)
    for mask in (1, 2, 4):
        query_part(mask)
    loss_swap.wait_recv()
    loss_plane[place, :, :] = jnp.sum(loss_core[...], axis=0)
    loss_copies = [links.copy(loss_plane.at[place], loss_plane.at[place], device) for device in plane.values()]
    queries.back(6, 0, 7)
    queries.back(3, 1, 7)
    key_part(0)
    keys.back(1, 0, 5)
    keys.back(2, 0, 3)
    keys.back(4, 1, 6)
    keys.back(1, 1, 5)
    query_part(0)
    for mask in (1, 2, 4):
        sib[mask].wait_recv()
    queries.back(1, 0, 5)
    queries.back(2, 0, 3)
    queries.back(4, 1, 6)
    queries.back(1, 1, 5)
    keys.back(4, 0, 6)
    keys.back(2, 1, 3)
    queries.back(4, 0, 6)
    queries.back(2, 1, 3)
    sib[0].wait_recv()
    for copy in loss_copies:
        copy.wait_recv()
    loss_z[z, :, :] = jnp.sum(loss_plane[...], axis=0)
    loss_copies = [links.copy(loss_z.at[z], loss_z.at[z], device) for device in column.values()]

    for view, group in ((1, keys), (0, queries)):
        here = slice(view * ROWS, (view + 1) * ROWS)
        gradient = SCALE * (group.whole() - pos[here, :])
        normal = unit[here, :]
        along = jnp.sum(normal * gradient, axis=1, keepdims=True)
        gm[here, :] = (inv[here, 0:1] * (gradient - normal * along)).astype(BF16)
        small = nt(gm[here, :], up_ref[...])
        gl[here, :] = small.astype(BF16)
        small_rows = small.T.astype(BF16)

        def down_chunk(step, carry, here=here, small_rows=small_rows, view=view):
            columns = pl.ds(pl.multiple_of(step * 512, 512), 512)
            value = nn(small_rows, h[here, columns])
            if view == 0:
                value = value + gsum[:, columns]
                gsend[:, columns] = value.astype(BF16)
            gsum[:, columns] = value
            return carry

        lax.fori_loop(0, MODEL // 512, down_chunk, 0)
        value = tn(low[here, :], gm[here, :])
        if view == 0:
            value = value + gsum[:, MODEL:TOTAL]
            gsend[:, MODEL:TOTAL] = value.astype(BF16)
        gsum[:, MODEL:TOTAL] = value

    mine = pl.ds(pl.multiple_of(core * HALF_RANK, HALF_RANK), HALF_RANK)
    theirs = pl.ds(pl.multiple_of((1 - core) * HALF_RANK, HALF_RANK), HALF_RANK)
    core_got = links.copy(gsend.at[theirs], core_in, sibling)
    for copy in loss_copies:
        copy.wait_recv()
    loss_ref[0, 0] = jnp.sum(jnp.sum(loss_z[...], axis=0)[0:1, 0:1]) * (1.0 / TEXTS) + SCALE
    core_got.wait_recv()
    for piece in range(16):
        top, side = (piece // 8) * 16, (piece % 8) * PIECE
        columns = slice(side, side + PIECE)
        value = gsum[pl.ds(pl.multiple_of(core * HALF_RANK + top, 16), 16), columns]
        value = value + core_in[top : top + 16, columns].astype(F32)
        plane_out[piece, :, :] = value.astype(BF16)
    plane_got = []
    for (dx, dy), device in plane.items():
        there = lax.rem(x + dx, 4) * 4 + lax.rem(y + dy, 4)
        plane_got.append(links.copy(plane_out.at[there], plane_in.at[place], device))
    plane_in[place, :, :] = plane_out[place]
    for copy in plane_got:
        copy.wait_recv()
    z_all[z, :, :] = jnp.sum(plane_in[...].astype(F32), axis=0).astype(BF16)
    z_got = [links.copy(z_all.at[z], z_all.at[z], device) for device in column.values()]
    for copy in z_got:
        copy.wait_recv()
    sums[core, place, :, :] = jnp.sum(z_all[...].astype(F32), axis=0).astype(BF16)
    plane_back = {step: links.copy(sums.at[core, place], sums.at[core, place], device) for step, device in plane.items()}
    core_back = [links.copy(sums.at[core, place], sums.at[core, place], sibling)]
    for (dx, dy), copy in plane_back.items():
        copy.wait_recv()
        came = lax.rem(x + 4 - dx, 4) * 4 + lax.rem(y + 4 - dy, 4)
        core_back.append(links.copy(sums.at[core, came], sums.at[core, came], sibling))
    for copy in core_back:
        copy.wait_recv()
    links.drain()


def finish(
    loss_in, gl, gm, sums, down, loss_out, g1_hbm, g2_hbm, gdown_hbm, gup_hbm, state, grad_down, grad_up, sems
):
    loss_out[0, 0] = loss_in[0, 0]
    copies = []
    for view, target in enumerate((g1_hbm, g2_hbm)):
        here = slice(view * ROWS, (view + 1) * ROWS)
        value = nn(gl[here, :], down[:, 0:WIDTH]) + gm[here, :].astype(F32)
        state[view, :, 0:WIDTH] = value.astype(BF16)

        def chunk(step, carry, here=here, view=view):
            columns = pl.ds(pl.multiple_of(WIDTH + step * 1024, 1024), 1024)
            state[view, :, columns] = nn(gl[here, :], down[:, columns]).astype(BF16)
            return carry

        lax.fori_loop(0, MODEL // WIDTH - 1, chunk, 0)
        copies.append(pltpu.make_async_copy(state.at[view], target, sems.at[view]))
        copies[-1].start()
    for rank in range(2):
        for piece in range(16):
            top, first = rank * HALF_RANK + (piece // 8) * 16, (piece % 8) * PIECE
            last = first + PIECE
            value = sums[rank, piece].astype(F32)
            rows = slice(top, top + 16)
            if last <= MODEL:
                grad_down[rows, first:last] = value
            elif first < MODEL:
                grad_down[rows, first:MODEL] = value[:, 0 : MODEL - first]
                grad_up[rows, 0 : last - MODEL] = value[:, MODEL - first :]
            else:
                grad_up[rows, first - MODEL : last - MODEL] = value
    for source, target, index in ((grad_down, gdown_hbm, 2), (grad_up, gup_hbm, 3)):
        copies.append(pltpu.make_async_copy(source, target, sems.at[index]))
        copies[-1].start()
    for copy in copies:
        copy.wait()


def shards(first_pooled_view, second_pooled_view, partner, adapter_down_weight, adapter_up_weight):
    vmem, hbm = pl.BlockSpec(memory_space=pltpu.VMEM), pl.BlockSpec(memory_space=pl.ANY)
    smem = pl.BlockSpec(memory_space=pltpu.SMEM)
    down_rows = adapter_down_weight.T
    loss, small, mixed, sums = pl.pallas_call(
        body,
        out_shape=(
            jax.ShapeDtypeStruct((1, 1), F32),
            jax.ShapeDtypeStruct((2 * ROWS, RANK), BF16),
            jax.ShapeDtypeStruct((2 * ROWS, WIDTH), BF16),
            jax.ShapeDtypeStruct((2, 16, 16, PIECE), BF16),
        ),
        in_specs=[hbm, hbm, vmem, hbm, vmem],
        out_specs=(smem, vmem, vmem, vmem),
        scratch_shapes=[
            pltpu.VMEM((2 * ROWS, MODEL), BF16),
            pltpu.VMEM((RANK, MODEL), BF16),
            pltpu.VMEM((2 * ROWS, WIDTH), F32),
            pltpu.VMEM((2 * ROWS, LANES), F32),
            pltpu.VMEM((2 * ROWS, RANK), BF16),
            pltpu.VMEM((16 * ROWS, WIDTH), BF16),
            pltpu.VMEM((8 * ROWS, WIDTH), BF16),
            pltpu.VMEM((16 * ROWS, 8 * ROWS), F32),
            pltpu.VMEM((16 * ROWS, LANES), F32),
            pltpu.VMEM((8, 8 * ROWS), F32),
            pltpu.VMEM((16, LANES), F32),
            pltpu.VMEM((8, LANES), F32),
            pltpu.VMEM((7, 16, LANES), F32),
            pltpu.VMEM((16, LANES), F32),
            pltpu.VMEM((7, 8, LANES), F32),
            pltpu.VMEM((16 * ROWS, 8 * ROWS), BF16),
            pltpu.VMEM((8, 8 * ROWS), F32),
            pltpu.VMEM((8, ROWS, WIDTH), F32),
            pltpu.VMEM((8 * ROWS, WIDTH), F32),
            pltpu.VMEM((8, ROWS, WIDTH), BF16),
            pltpu.VMEM((8, ROWS, WIDTH), BF16),
            pltpu.VMEM((7, ROWS, WIDTH), BF16),
            pltpu.VMEM((7, ROWS, WIDTH), BF16),
            pltpu.VMEM((7, ROWS, WIDTH), BF16),
            pltpu.VMEM((7, ROWS, WIDTH), BF16),
            pltpu.VMEM((2 * ROWS, WIDTH), F32),
            pltpu.VMEM((RANK, TOTAL), F32),
            pltpu.VMEM((RANK, TOTAL), BF16),
            pltpu.VMEM((HALF_RANK, TOTAL), BF16),
            pltpu.VMEM((16, 16, PIECE), BF16),
            pltpu.VMEM((16, 16, PIECE), BF16),
            pltpu.VMEM((4, 16, PIECE), BF16),
            pltpu.VMEM((2, 8, LANES), F32),
            pltpu.VMEM((16, 8, LANES), F32),
            pltpu.VMEM((4, 8, LANES), F32),
            pltpu.SemaphoreType.DMA((3,)),
            pltpu.SemaphoreType.DMA((COPIES,)),
            pltpu.SemaphoreType.DMA((COPIES,)),
        ],
        compiler_params=pltpu.CompilerParams(
            collective_id=0, has_side_effects=True, vmem_limit_bytes=60 * 1024 * 1024
        ),
    )(first_pooled_view, second_pooled_view, partner, down_rows, adapter_up_weight)
    loss, first_gradient, second_gradient, grad_down, grad_up = pl.pallas_call(
        finish,
        out_shape=(
            jax.ShapeDtypeStruct((1, 1), F32),
            jax.ShapeDtypeStruct((ROWS, MODEL), BF16),
            jax.ShapeDtypeStruct((ROWS, MODEL), BF16),
            jax.ShapeDtypeStruct((RANK, MODEL), F32),
            jax.ShapeDtypeStruct((RANK, WIDTH), F32),
        ),
        in_specs=[smem, vmem, vmem, vmem, vmem],
        out_specs=(smem, hbm, hbm, hbm, hbm),
        scratch_shapes=[
            pltpu.VMEM((2, ROWS, MODEL), BF16),
            pltpu.VMEM((RANK, MODEL), F32),
            pltpu.VMEM((RANK, WIDTH), F32),
            pltpu.SemaphoreType.DMA((4,)),
        ],
        compiler_params=pltpu.CompilerParams(vmem_limit_bytes=32 * 1024 * 1024),
    )(loss, small, mixed, sums, down_rows)
    return (loss[0, 0], first_gradient, second_gradient, grad_down.T, grad_up)


def solution(mesh):
    in_specs = (P(("blk", "grp"), None), P(("blk", "grp"), None), P(("blk", "grp"), None), P(), P())
    out_specs = (P(), P(("blk", "grp"), None), P(("blk", "grp"), None), P(), P())
    return jax.shard_map(shards, mesh=mesh, in_specs=in_specs, out_specs=out_specs, check_vma=False)
```

time: 112 us -> 96.3 us (0.86)
  Pallas kernels: 104 us -> 92.4 us
  local copies, waits for them, and re-layouts: 6.96 us -> 2.96 us
    pallas_call x1 -> x2, Pallas kernels: 104 us -> 92.4 us  [the longest x1 88.2 us: shards(): pl.pallas_call(body, out_shape=(jax.ShapeDtypeStruct((1, 1), F32), jax.Sh...]
    unnamed x10 -> x8, local copies, waits for them, and re-layouts: 5.77 us -> 2.96 us
    slice x1 -> x0, local copies, waits for them, and re-layouts: 1.19 us -> none  [shards(): return (loss[0, 0], first_gradient, second_gradient, down_rows.T, grad_up)]
where the time goes in v2:
time: 96.3 us; the launch traced here: 96 us
  Pallas kernels  92.4 us (96%)
  local copies, waits for them, and re-layouts  2.96 us (3%)
    pallas_call x1, Pallas kernels, shards(): pl.pallas_call(body, out_shape=(jax.ShapeDtypeStruct((1, 1), F32), jax.Sh...  88.2 us
    pallas_call x1, Pallas kernels, shards(): pl.pallas_call(finish, out_shape=(jax.ShapeDtypeStruct((1, 1), F32), jax....  4.23 us
    unnamed x8, local copies, waits for them, and re-layouts  2.96 us

profile of v2, /device:TPU:1, one launch (start us, length us, event | category | flops | bytes accessed | tf_op | source)
XLA Modules:
  0.0 96.0 jit_solution(17594061796735396803)
XLA Ops:
  0.6 0.0 copy-start
  0.6 88.2 %shard_map.92 = (f32[1,1]{1,0:T(1,128)}, bf16[256,64]{1,0:T(8,128)(2,1)}, bf16[256,1024]{1,0:T(8,128)(2,1)}, bf16[2,16,16,640]{3,2,1,0:T(8,128)(2,1)}) custom-call(bf16[128,4096]{1,0:T(8,128)(2,1)} %h1_hbm.1, bf16[128,4096]{1,0:T(8,128)(2,1)} %h2_hbm.1, s32[1,128]{1,0:T(1,128)} %partner_ref.1, bf16[64,4096]{1,0:T(8,128)(2,1)} %bitcast.3, bf16[64,1024]{1,0:T(8,128)(2,1)} %up_ref.1), custom_call_target="tpu_custom_call" | custom-call | tf_op jit(solution)/shard_map/pallas_call | solution.py:467
  88.8 0.0 copy-done
  88.8 0.0 copy-start.1
  88.8 1.1 %copy-done.1 = bf16[2,16,16,640]{3,2,1,0:T(8,128)(2,1)S(1)} copy-done((bf16[2,16,16,640]{3,2,1,0:T(8,128)(2,1)S(1)}, bf16[2,16,16,640]{3,2,1,0:T(8,128)(2,1)}, u32[]{:S(2)}) %copy-start.1) | copy-done | bytes 655384
  89.9 0.0 copy-start.2
  89.9 1.0 %copy-done.2 = bf16[256,1024]{1,0:T(8,128)(2,1)S(1)} copy-done((bf16[256,1024]{1,0:T(8,128)(2,1)S(1)}, bf16[256,1024]{1,0:T(8,128)(2,1)}, u32[]{:S(2)}) %copy-start.2) | copy-done | bytes 524312
  90.9 0.0 copy-start.3
  91.0 0.8 copy-done.3
  91.8 4.2 %shard_map.93 = (f32[1,1]{1,0:T(1,128)}, bf16[128,4096]{1,0:T(8,128)(2,1)}, bf16[128,4096]{1,0:T(8,128)(2,1)}, f32[64,4096]{1,0:T(8,128)}, f32[64,1024]{1,0:T(8,128)}) custom-call(f32[1,1]{1,0:T(1,128)} %get-tuple-element.14.loss_in, bf16[256,64]{1,0:T(8,128)(2,1)S(1)} %copy-done.3, bf16[256,1024]{1,0:T(8,128)(2,1)S(1)} %copy-done.2, ...), custom_call_target="tpu_custom_call" | custom-call | tf_op jit(solution)/shard_map/pallas_call | solution.py:521
Async XLA Ops:
  0.6 88.2 %copy-start = (bf16[4096,64]{0,1:T(8,128)(2,1)S(1)}, bf16[4096,64]{0,1:T(8,128)(2,1)}, u32[]{:S(2)}) copy-start(bf16[4096,64]{0,1:T(8,128)(2,1)} %param.8) | copy-start | bytes 1572868
  88.8 1.1 %copy-start.1 = (bf16[2,16,16,640]{3,2,1,0:T(8,128)(2,1)S(1)}, bf16[2,16,16,640]{3,2,1,0:T(8,128)(2,1)}, u32[]{:S(2)}) copy-start(bf16[2,16,16,640]{3,2,1,0:T(8,128)(2,1)} %get-tuple-element.17.sums) | copy-start | bytes 1966084
  89.9 1.0 %copy-start.2 = (bf16[256,1024]{1,0:T(8,128)(2,1)S(1)}, bf16[256,1024]{1,0:T(8,128)(2,1)}, u32[]{:S(2)}) copy-start(bf16[256,1024]{1,0:T(8,128)(2,1)} %get-tuple-element.16.gm) | copy-start | bytes 1572868
  90.9 0.8 copy-start.3

commit v3 on v2

--- a/solution.py
+++ b/solution.py
@@ -113,11 +113,11 @@
 
 
 def body(
-    h1_hbm, h2_hbm, partner_ref, down_hbm, up_ref,
-    loss_ref, gl, gm, sums,
-    h, down, unit, inv, low, q, k, expo, rowacc, colacc, rows, cols, row_in, row_sib_in, col_in,
+    h1_hbm, h2_hbm, partner_hbm, down_hbm, up_hbm,
+    loss_ref, g1_hbm, g2_hbm, sums_hbm,
+    h, down, up_ref, partner_ref, unit, inv, low, q, k, expo, rowacc, colacc, rows, cols, row_in, row_sib_in, col_in,
     w, colb, pq, pk, sib_out, sib_in, q_out, q_in, k_out, k_in, pos,
-    gsum, gsend, core_in, plane_out, plane_in, z_all,
+    gl, gm, state, gsum, gsend, core_in, plane_out, plane_in, z_all, sums,
     loss_core, loss_plane, loss_z,
     load_sems, send_sems, recv_sems,
 ):
@@ -148,11 +148,12 @@
         pltpu.make_async_copy(h1_hbm, h.at[0:ROWS], load_sems.at[0]),
         pltpu.make_async_copy(h2_hbm, h.at[ROWS : 2 * ROWS], load_sems.at[1]),
         pltpu.make_async_copy(down_hbm, down, load_sems.at[2]),
+        pltpu.make_async_copy(up_hbm, up_ref, load_sems.at[3]),
+        pltpu.make_async_copy(partner_hbm, partner_ref, load_sems.at[4]),
     ]
     for load in loads:
         load.start()
-    partners = [sibling, *plane.values(), *column.values()]
-    partners += [near[m] for near in (q_near, k_near) for m in (5, 6, 7)]
+    partners = [sibling, *(near[m] for near in (q_near, k_near) for m in (1, 2, 4))]
     barrier = pltpu.get_barrier_semaphore()
     for device in partners:
         pl.semaphore_signal(barrier, inc=1, device_id=device, device_id_type=MESH)
@@ -404,42 +405,51 @@
         there = lax.rem(x + dx, 4) * 4 + lax.rem(y + dy, 4)
         plane_got.append(links.copy(plane_out.at[there], plane_in.at[place], device))
     plane_in[place, :, :] = plane_out[place]
+    stores = []
+    for view, target in enumerate((g1_hbm, g2_hbm)):
+        here = slice(view * ROWS, (view + 1) * ROWS)
+        state[view, :, 0:WIDTH] = (nn(gl[here, :], down[:, 0:WIDTH]) + gm[here, :].astype(F32)).astype(BF16)
+
+        def chunk(step, carry, here=here, view=view):
+            columns = pl.ds(pl.multiple_of(WIDTH + step * 512, 512), 512)
+            state[view, :, columns] = nn(gl[here, :], down[:, columns]).astype(BF16)
+            return carry
+
+        lax.fori_loop(0, (MODEL - WIDTH) // 512, chunk, 0)
+        stores.append(pltpu.make_async_copy(state.at[view], target, load_sems.at[view]))
+        stores[-1].start()
     for copy in plane_got:
         copy.wait_recv()
     z_all[z, :, :] = jnp.sum(plane_in[...].astype(F32), axis=0).astype(BF16)
     z_got = [links.copy(z_all.at[z], z_all.at[z], device) for device in column.values()]
     for copy in z_got:
         copy.wait_recv()
-    sums[core, place, :, :] = jnp.sum(z_all[...].astype(F32), axis=0).astype(BF16)
-    plane_back = {step: links.copy(sums.at[core, place], sums.at[core, place], device) for step, device in plane.items()}
-    core_back = [links.copy(sums.at[core, place], sums.at[core, place], sibling)]
+    sums[place, :, :] = jnp.sum(z_all[...].astype(F32), axis=0).astype(BF16)
+    plane_back = {step: links.copy(sums.at[place], sums.at[place], device) for step, device in plane.items()}
+    core_back = [links.copy(sums.at[place], sums_hbm.at[core, place], sibling)]
     for (dx, dy), copy in plane_back.items():
         copy.wait_recv()
         came = lax.rem(x + 4 - dx, 4) * 4 + lax.rem(y + 4 - dy, 4)
-        core_back.append(links.copy(sums.at[core, came], sums.at[core, came], sibling))
+        core_back.append(links.copy(sums.at[came], sums_hbm.at[core, came], sibling))
+    stores.append(pltpu.make_async_copy(sums, sums_hbm.at[core], load_sems.at[2]))
+    stores[-1].start()
     for copy in core_back:
         copy.wait_recv()
+    for store in stores:
+        store.wait()
     links.drain()
 
 
 def finish(
-    loss_in, gl, gm, sums, down, loss_out, g1_hbm, g2_hbm, gdown_hbm, gup_hbm, state, grad_down, grad_up, sems
+    loss_in, g1_in, g2_in, sums_in, loss_out, g1_out, g2_out, gdown_out, gup_out, sums, grad_down, grad_up, sems
 ):
+    load = pltpu.make_async_copy(sums_in, sums, sems.at[0])
+    load.start()
+    copies = [pltpu.make_async_copy(g1_in, g1_out, sems.at[1]), pltpu.make_async_copy(g2_in, g2_out, sems.at[2])]
+    for copy in copies:
+        copy.start()
     loss_out[0, 0] = loss_in[0, 0]
-    copies = []
-    for view, target in enumerate((g1_hbm, g2_hbm)):
-        here = slice(view * ROWS, (view + 1) * ROWS)
-        value = nn(gl[here, :], down[:, 0:WIDTH]) + gm[here, :].astype(F32)
-        state[view, :, 0:WIDTH] = value.astype(BF16)
-
-        def chunk(step, carry, here=here, view=view):
-            columns = pl.ds(pl.multiple_of(WIDTH + step * 1024, 1024), 1024)
-            state[view, :, columns] = nn(gl[here, :], down[:, columns]).astype(BF16)
-            return carry
-
-        lax.fori_loop(0, MODEL // WIDTH - 1, chunk, 0)
-        copies.append(pltpu.make_async_copy(state.at[view], target, sems.at[view]))
-        copies[-1].start()
+    load.wait()
     for rank in range(2):
         for piece in range(16):
             top, first = rank * HALF_RANK + (piece // 8) * 16, (piece % 8) * PIECE
@@ -453,7 +463,7 @@
                 grad_up[rows, 0 : last - MODEL] = value[:, MODEL - first :]
             else:
                 grad_up[rows, first - MODEL : last - MODEL] = value
-    for source, target, index in ((grad_down, gdown_hbm, 2), (grad_up, gup_hbm, 3)):
+    for source, target, index in ((grad_down, gdown_out, 3), (grad_up, gup_out, 4)):
         copies.append(pltpu.make_async_copy(source, target, sems.at[index]))
         copies[-1].start()
     for copy in copies:
@@ -461,22 +471,24 @@
 
 
 def shards(first_pooled_view, second_pooled_view, partner, adapter_down_weight, adapter_up_weight):
-    vmem, hbm = pl.BlockSpec(memory_space=pltpu.VMEM), pl.BlockSpec(memory_space=pl.ANY)
+    hbm = pl.BlockSpec(memory_space=pl.ANY)
     smem = pl.BlockSpec(memory_space=pltpu.SMEM)
     down_rows = adapter_down_weight.T
-    loss, small, mixed, sums = pl.pallas_call(
+    loss, first_state, second_state, sums = pl.pallas_call(
         body,
         out_shape=(
             jax.ShapeDtypeStruct((1, 1), F32),
-            jax.ShapeDtypeStruct((2 * ROWS, RANK), BF16),
-            jax.ShapeDtypeStruct((2 * ROWS, WIDTH), BF16),
+            jax.ShapeDtypeStruct((ROWS, MODEL), BF16),
+            jax.ShapeDtypeStruct((ROWS, MODEL), BF16),
             jax.ShapeDtypeStruct((2, 16, 16, PIECE), BF16),
         ),
-        in_specs=[hbm, hbm, vmem, hbm, vmem],
-        out_specs=(smem, vmem, vmem, vmem),
+        in_specs=[hbm, hbm, hbm, hbm, hbm],
+        out_specs=(smem, hbm, hbm, hbm),
         scratch_shapes=[
             pltpu.VMEM((2 * ROWS, MODEL), BF16),
             pltpu.VMEM((RANK, MODEL), BF16),
+            pltpu.VMEM((RANK, WIDTH), BF16),
+            pltpu.VMEM((1, ROWS), jnp.int32),
             pltpu.VMEM((2 * ROWS, WIDTH), F32),
             pltpu.VMEM((2 * ROWS, LANES), F32),
             pltpu.VMEM((2 * ROWS, RANK), BF16),
@@ -501,16 +513,20 @@
             pltpu.VMEM((7, ROWS, WIDTH), BF16),
             pltpu.VMEM((7, ROWS, WIDTH), BF16),
             pltpu.VMEM((2 * ROWS, WIDTH), F32),
+            pltpu.VMEM((2 * ROWS, RANK), BF16),
+            pltpu.VMEM((2 * ROWS, WIDTH), BF16),
+            pltpu.VMEM((2, ROWS, MODEL), BF16),
             pltpu.VMEM((RANK, TOTAL), F32),
             pltpu.VMEM((RANK, TOTAL), BF16),
             pltpu.VMEM((HALF_RANK, TOTAL), BF16),
             pltpu.VMEM((16, 16, PIECE), BF16),
             pltpu.VMEM((16, 16, PIECE), BF16),
             pltpu.VMEM((4, 16, PIECE), BF16),
+            pltpu.VMEM((16, 16, PIECE), BF16),
             pltpu.VMEM((2, 8, LANES), F32),
             pltpu.VMEM((16, 8, LANES), F32),
             pltpu.VMEM((4, 8, LANES), F32),
-            pltpu.SemaphoreType.DMA((3,)),
+            pltpu.SemaphoreType.DMA((5,)),
             pltpu.SemaphoreType.DMA((COPIES,)),
             pltpu.SemaphoreType.DMA((COPIES,)),
         ],
@@ -527,16 +543,16 @@
             jax.ShapeDtypeStruct((RANK, MODEL), F32),
             jax.ShapeDtypeStruct((RANK, WIDTH), F32),
         ),
-        in_specs=[smem, vmem, vmem, vmem, vmem],
+        in_specs=[smem, hbm, hbm, hbm],
         out_specs=(smem, hbm, hbm, hbm, hbm),
         scratch_shapes=[
-            pltpu.VMEM((2, ROWS, MODEL), BF16),
+            pltpu.VMEM((2, 16, 16, PIECE), BF16),
             pltpu.VMEM((RANK, MODEL), F32),
             pltpu.VMEM((RANK, WIDTH), F32),
-            pltpu.SemaphoreType.DMA((4,)),
+            pltpu.SemaphoreType.DMA((5,)),
         ],
-        compiler_params=pltpu.CompilerParams(vmem_limit_bytes=32 * 1024 * 1024),
-    )(loss, small, mixed, sums, down_rows)
+        compiler_params=pltpu.CompilerParams(vmem_limit_bytes=60 * 1024 * 1024),
+    )(loss, first_state, second_state, sums)
     return (loss[0, 0], first_gradient, second_gradient, grad_down.T, grad_up)
 
 

time: 96.3 us -> 153 us (1.59)
  Pallas kernels: 92.4 us -> 152 us
  local copies, waits for them, and re-layouts: 2.96 us -> 0 us
    pallas_call x1, Pallas kernels: 4.23 us -> 65.9 us  [shards(): pl.pallas_call(finish, out_shape=(jax.ShapeDtypeStruct((1, 1), F32), jax....]
    unnamed x8 -> x0, local copies, waits for them, and re-layouts: 2.96 us -> none
    pallas_call x1, Pallas kernels: 88.2 us -> 86.1 us  [shards(): pl.pallas_call(body, out_shape=(jax.ShapeDtypeStruct((1, 1), F32), jax.Sh...]
where the time goes in v3:
time: 153 us
  Pallas kernels  152 us (99%)
    pallas_call x1, Pallas kernels, shards(): pl.pallas_call(body, out_shape=(jax.ShapeDtypeStruct((1, 1), F32), jax.Sh...  86.1 us
    pallas_call x1, Pallas kernels, shards(): pl.pallas_call(finish, out_shape=(jax.ShapeDtypeStruct((1, 1), F32), jax....  65.9 us

profile of v3, /device:TPU:1, one launch (start us, length us, event | category | flops | bytes accessed | tf_op | source)
XLA Modules:
  0.0 152.6 jit_solution(10033786585679797084)
XLA Ops:
  0.6 86.1 %shard_map.92 = (f32[1,1]{1,0:T(1,128)}, bf16[128,4096]{1,0:T(8,128)(2,1)}, bf16[128,4096]{1,0:T(8,128)(2,1)}, bf16[2,16,16,640]{3,2,1,0:T(8,128)(2,1)}) custom-call(bf16[128,4096]{1,0:T(8,128)(2,1)} %h1_hbm.1, bf16[128,4096]{1,0:T(8,128)(2,1)} %h2_hbm.1, s32[1,128]{1,0:T(1,128)} %partner_hbm.1, bf16[64,4096]{1,0:T(8,128)(2,1)} %bitcast.3, ...), custom_call_target="tpu_custom_call" | custom-call | tf_op jit(solution)/shard_map/pallas_call | solution.py:477
  86.7 65.9 %shard_map.93 = (f32[1,1]{1,0:T(1,128)}, bf16[128,4096]{1,0:T(8,128)(2,1)}, bf16[128,4096]{1,0:T(8,128)(2,1)}, f32[64,4096]{1,0:T(8,128)}, f32[64,1024]{1,0:T(8,128)}) custom-call(f32[1,1]{1,0:T(1,128)} %get-tuple-element.14.loss_in, bf16[128,4096]{1,0:T(8,128)(2,1)} %get-tuple-element.15.g1_in, bf16[128,4096]{1,0:T(8,128)(2,1)} %get-tuple-element.16.g2_in, ...), custom_call_target="tpu_custom_call" | custom-call | tf_op jit(solution)/shard_map/pallas_call | solution.py:537

commit v4 on v3

--- a/solution.py
+++ b/solution.py
@@ -206,19 +206,16 @@
         passed[mask] = to_sibling(mask)
 
     def score(first_row, row_count, first_col, col_count):
-        def chunk(step, carry):
-            here = pl.ds(pl.multiple_of(first_row + step * 256, 256), 256)
-            columns = pl.ds(first_col, col_count)
+        columns = slice(first_col, first_col + col_count)
+        for top in range(first_row, first_row + row_count, 512):
+            here = slice(top, min(top + 512, first_row + row_count))
             value = jnp.exp(SCALE * nt(q[here, :], k[columns, :]) - SCALE)
             expo[here, columns] = value
-            colacc[:, columns] += jnp.sum(value.reshape(32, 8, col_count), axis=0)
+            colacc[:, columns] += jnp.sum(value.reshape(-1, 8, col_count), axis=0)
             total = value[:, 0:LANES]
             for lane in range(LANES, col_count, LANES):
                 total = total + value[:, lane : lane + LANES]
             rowacc[here, :] += total
-            return carry
-
-        lax.fori_loop(0, row_count // 256, chunk, 0)
 
     for mask in (0, 1, 2, 4):
         passed[mask].wait_recv()
@@ -285,15 +282,17 @@
     for slot, value in enumerate(sums_of_rows):
         rows[2 * slot : 2 * slot + 2, :] = 0.5 / value
 
-    def weigh(block, carry):
-        here = pl.ds(pl.multiple_of(block * ROWS, ROWS), ROWS)
-        row = jnp.broadcast_to(rows[pl.ds(block, 1), :], (ROWS, ROWS)).T
-        for lane in range(0, WIDTH, LANES):
-            columns = slice(lane, lane + LANES)
-            w[here, columns] = (expo[here, columns] * (row + colb[0:1, columns])).astype(BF16)
+    def weigh(step, carry):
+        for part in range(2):
+            block = step * 2 + part
+            here = pl.ds(pl.multiple_of(block * ROWS, ROWS), ROWS)
+            row = jnp.broadcast_to(rows[pl.ds(block, 1), :], (ROWS, ROWS)).T
+            for lane in range(0, WIDTH, LANES):
+                columns = slice(lane, lane + LANES)
+                w[here, columns] = (expo[here, columns] * (row + colb[0:1, columns])).astype(BF16)
         return carry
 
-    lax.fori_loop(0, 16, weigh, 0)
+    lax.fori_loop(0, 8, weigh, 0)
 
     def key_part(first):
         pk[first : first + 256, :] = tn(w[:, first : first + 256], q[...])
@@ -306,18 +305,18 @@
         sib_out[slot, :, :] = part[ROWS:].astype(BF16)
         sib[mask] = links.copy(sib_out.at[slot], sib_in.at[slot], sibling)
 
+    query_part(7)
     key_part(768)
     for mask, half in ((7, 0), (7, 1), (5, 0), (5, 1)):
         keys.back(mask, half)
-    query_part(7)
-    key_part(512)
-    keys.back(3, 0)
-    keys.back(6, 1)
     sib[7].wait_recv()
     queries.back(7, 0)
     queries.back(7, 1)
     for mask in (5, 3, 6):
         query_part(mask)
+    key_part(512)
+    keys.back(3, 0)
+    keys.back(6, 1)
     sib[5].wait_recv()
     queries.back(5, 0)
     queries.back(5, 1)
@@ -326,40 +325,27 @@
     sib[6].wait_recv()
     queries.back(6, 1)
 
+    key_part(256)
+    keys.back(6, 0, 7)
+    keys.back(3, 1, 7)
+    queries.back(6, 0, 7)
+    queries.back(3, 1, 7)
+    for mask in (1, 2, 4):
+        query_part(mask)
+    key_part(0)
+    for mask in (1, 2, 4):
+        sib[mask].wait_recv()
+    for mask, half, add in ((1, 0, 5), (2, 0, 3), (4, 1, 6), (1, 1, 5), (4, 0, 6), (2, 1, 3)):
+        for group in groups:
+            group.back(mask, half, add)
+    query_part(0)
+
     terms = 0.5 * jnp.sum(jnp.log(sums_of_rows[0][0:1, :])) + 0.5 * jnp.sum(jnp.log(sums_of_cols[0])) - positive
     loss_core[core, :, :] = jnp.broadcast_to(terms, (8, LANES))
     loss_swap = links.copy(loss_core.at[core], loss_core.at[core], sibling)
-    key_part(256)
-    keys.back(6, 0, 7)
-    keys.back(3, 1, 7)
-    for mask in (1, 2, 4):
-        query_part(mask)
     loss_swap.wait_recv()
     loss_plane[place, :, :] = jnp.sum(loss_core[...], axis=0)
-    loss_copies = [links.copy(loss_plane.at[place], loss_plane.at[place], device) for device in plane.values()]
-    queries.back(6, 0, 7)
-    queries.back(3, 1, 7)
-    key_part(0)
-    keys.back(1, 0, 5)
-    keys.back(2, 0, 3)
-    keys.back(4, 1, 6)
-    keys.back(1, 1, 5)
-    query_part(0)
-    for mask in (1, 2, 4):
-        sib[mask].wait_recv()
-    queries.back(1, 0, 5)
-    queries.back(2, 0, 3)
-    queries.back(4, 1, 6)
-    queries.back(1, 1, 5)
-    keys.back(4, 0, 6)
-    keys.back(2, 1, 3)
-    queries.back(4, 0, 6)
-    queries.back(2, 1, 3)
     sib[0].wait_recv()
-    for copy in loss_copies:
-        copy.wait_recv()
-    loss_z[z, :, :] = jnp.sum(loss_plane[...], axis=0)
-    loss_copies = [links.copy(loss_z.at[z], loss_z.at[z], device) for device in column.values()]
 
     for view, group in ((1, keys), (0, queries)):
         here = slice(view * ROWS, (view + 1) * ROWS)
@@ -370,29 +356,17 @@
         small = nt(gm[here, :], up_ref[...])
         gl[here, :] = small.astype(BF16)
         small_rows = small.T.astype(BF16)
-
-        def down_chunk(step, carry, here=here, small_rows=small_rows, view=view):
-            columns = pl.ds(pl.multiple_of(step * 512, 512), 512)
-            value = nn(small_rows, h[here, columns])
+        for first in range(0, TOTAL, WIDTH):
+            columns = slice(first, first + WIDTH)
+            value = nn(small_rows, h[here, columns]) if first < MODEL else tn(low[here, :], gm[here, :])
             if view == 0:
                 value = value + gsum[:, columns]
                 gsend[:, columns] = value.astype(BF16)
             gsum[:, columns] = value
-            return carry
-
-        lax.fori_loop(0, MODEL // 512, down_chunk, 0)
-        value = tn(low[here, :], gm[here, :])
-        if view == 0:
-            value = value + gsum[:, MODEL:TOTAL]
-            gsend[:, MODEL:TOTAL] = value.astype(BF16)
-        gsum[:, MODEL:TOTAL] = value
 
     mine = pl.ds(pl.multiple_of(core * HALF_RANK, HALF_RANK), HALF_RANK)
     theirs = pl.ds(pl.multiple_of((1 - core) * HALF_RANK, HALF_RANK), HALF_RANK)
     core_got = links.copy(gsend.at[theirs], core_in, sibling)
-    for copy in loss_copies:
-        copy.wait_recv()
-    loss_ref[0, 0] = jnp.sum(jnp.sum(loss_z[...], axis=0)[0:1, 0:1]) * (1.0 / TEXTS) + SCALE
     core_got.wait_recv()
     for piece in range(16):
         top, side = (piece // 8) * 16, (piece % 8) * PIECE
@@ -405,6 +379,7 @@
         there = lax.rem(x + dx, 4) * 4 + lax.rem(y + dy, 4)
         plane_got.append(links.copy(plane_out.at[there], plane_in.at[place], device))
     plane_in[place, :, :] = plane_out[place]
+    loss_got = [links.copy(loss_plane.at[place], loss_plane.at[place], device) for device in plane.values()]
     stores = []
     for view, target in enumerate((g1_hbm, g2_hbm)):
         here = slice(view * ROWS, (view + 1) * ROWS)
@@ -422,11 +397,18 @@
         copy.wait_recv()
     z_all[z, :, :] = jnp.sum(plane_in[...].astype(F32), axis=0).astype(BF16)
     z_got = [links.copy(z_all.at[z], z_all.at[z], device) for device in column.values()]
+    for copy in loss_got:
+        copy.wait_recv()
+    loss_z[z, :, :] = jnp.sum(loss_plane[...], axis=0)
+    loss_got = [links.copy(loss_z.at[z], loss_z.at[z], device) for device in column.values()]
     for copy in z_got:
         copy.wait_recv()
     sums[place, :, :] = jnp.sum(z_all[...].astype(F32), axis=0).astype(BF16)
     plane_back = {step: links.copy(sums.at[place], sums.at[place], device) for step, device in plane.items()}
     core_back = [links.copy(sums.at[place], sums_hbm.at[core, place], sibling)]
+    for copy in loss_got:
+        copy.wait_recv()
+    loss_ref[0, 0] = jnp.sum(jnp.sum(loss_z[...], axis=0)[0:1, 0:1]) * (1.0 / TEXTS) + SCALE
     for (dx, dy), copy in plane_back.items():
         copy.wait_recv()
         came = lax.rem(x + 4 - dx, 4) * 4 + lax.rem(y + 4 - dy, 4)
@@ -441,33 +423,43 @@
 
 
 def finish(
-    loss_in, g1_in, g2_in, sums_in, loss_out, g1_out, g2_out, gdown_out, gup_out, sums, grad_down, grad_up, sems
+    loss_in, g1_in, g2_in, sums_in, loss_out, g1_out, g2_out, gdown_out, gup_out, g1, g2, sums, grad_down, grad_up, sems
 ):
-    load = pltpu.make_async_copy(sums_in, sums, sems.at[0])
-    load.start()
-    copies = [pltpu.make_async_copy(g1_in, g1_out, sems.at[1]), pltpu.make_async_copy(g2_in, g2_out, sems.at[2])]
-    for copy in copies:
-        copy.start()
+    def copy(source, target, index):
+        made = pltpu.make_async_copy(source, target, sems.at[index])
+        made.start()
+        return made
+
+    first = copy(sums_in, sums, 0)
+    pieces = []
+    for source, buffer, target in ((g1_in, g1, g1_out), (g2_in, g2, g2_out)):
+        for top in range(0, ROWS, ROWS // 4):
+            here = pl.ds(top, ROWS // 4)
+            pieces.append((copy(source.at[here], buffer.at[here], 1 + len(pieces)), buffer.at[here], target.at[here]))
     loss_out[0, 0] = loss_in[0, 0]
-    load.wait()
+    stores = []
+    first.wait()
     for rank in range(2):
         for piece in range(16):
-            top, first = rank * HALF_RANK + (piece // 8) * 16, (piece % 8) * PIECE
-            last = first + PIECE
+            top, start = rank * HALF_RANK + (piece // 8) * 16, (piece % 8) * PIECE
+            last = start + PIECE
             value = sums[rank, piece].astype(F32)
             rows = slice(top, top + 16)
             if last <= MODEL:
-                grad_down[rows, first:last] = value
-            elif first < MODEL:
-                grad_down[rows, first:MODEL] = value[:, 0 : MODEL - first]
-                grad_up[rows, 0 : last - MODEL] = value[:, MODEL - first :]
+                grad_down[rows, start:last] = value
+            elif start < MODEL:
+                grad_down[rows, start:MODEL] = value[:, 0 : MODEL - start]
+                grad_up[rows, 0 : last - MODEL] = value[:, MODEL - start :]
             else:
-                grad_up[rows, first - MODEL : last - MODEL] = value
-    for source, target, index in ((grad_down, gdown_out, 3), (grad_up, gup_out, 4)):
-        copies.append(pltpu.make_async_copy(source, target, sems.at[index]))
-        copies[-1].start()
-    for copy in copies:
-        copy.wait()
+                grad_up[rows, start - MODEL : last - MODEL] = value
+        rows = pl.ds(rank * HALF_RANK, HALF_RANK)
+        stores.append(copy(grad_down.at[rows], gdown_out.at[rows], 17 + 2 * rank))
+        stores.append(copy(grad_up.at[rows], gup_out.at[rows], 18 + 2 * rank))
+    for index, (load, buffer, target) in enumerate(pieces):
+        load.wait()
+        stores.append(copy(buffer, target, 9 + index))
+    for store in stores:
+        store.wait()
 
 
 def shards(first_pooled_view, second_pooled_view, partner, adapter_down_weight, adapter_up_weight):
@@ -546,10 +538,12 @@
         in_specs=[smem, hbm, hbm, hbm],
         out_specs=(smem, hbm, hbm, hbm, hbm),
         scratch_shapes=[
+            pltpu.VMEM((ROWS, MODEL), BF16),
+            pltpu.VMEM((ROWS, MODEL), BF16),
             pltpu.VMEM((2, 16, 16, PIECE), BF16),
             pltpu.VMEM((RANK, MODEL), F32),
             pltpu.VMEM((RANK, WIDTH), F32),
-            pltpu.SemaphoreType.DMA((5,)),
+            pltpu.SemaphoreType.DMA((21,)),
         ],
         compiler_params=pltpu.CompilerParams(vmem_limit_bytes=60 * 1024 * 1024),
     )(loss, first_state, second_state, sums)

time: 153 us -> 87.9 us (0.57)
  Pallas kernels: 152 us -> 86.9 us
    pallas_call x1, Pallas kernels: 65.9 us -> 4.24 us  [shards(): pl.pallas_call(finish, out_shape=(jax.ShapeDtypeStruct((1, 1), F32), jax....]
    pallas_call x1, Pallas kernels: 86.1 us -> 82.6 us  [shards(): pl.pallas_call(body, out_shape=(jax.ShapeDtypeStruct((1, 1), F32), jax.Sh...]
where the time goes in v4:
time: 87.9 us; the launch traced here: 87.7 us
  Pallas kernels  86.9 us (99%)
    pallas_call x1, Pallas kernels, shards(): pl.pallas_call(body, out_shape=(jax.ShapeDtypeStruct((1, 1), F32), jax.Sh...  82.6 us
    pallas_call x1, Pallas kernels, shards(): pl.pallas_call(finish, out_shape=(jax.ShapeDtypeStruct((1, 1), F32), jax....  4.24 us

profile of v4, /device:TPU:1, one launch (start us, length us, event | category | flops | bytes accessed | tf_op | source)
XLA Modules:
  0.0 87.7 jit_solution(9025547888513107855)
XLA Ops:
  0.6 82.6 %shard_map.92 = (f32[1,1]{1,0:T(1,128)}, bf16[128,4096]{1,0:T(8,128)(2,1)}, bf16[128,4096]{1,0:T(8,128)(2,1)}, bf16[2,16,16,640]{3,2,1,0:T(8,128)(2,1)}) custom-call(bf16[128,4096]{1,0:T(8,128)(2,1)} %h1_hbm.1, bf16[128,4096]{1,0:T(8,128)(2,1)} %h2_hbm.1, s32[1,128]{1,0:T(1,128)} %partner_hbm.1, bf16[64,4096]{1,0:T(8,128)(2,1)} %bitcast.3, ...), custom_call_target="tpu_custom_call" | custom-call | tf_op jit(solution)/shard_map/pallas_call | solution.py:469
  83.3 4.2 %shard_map.93 = (f32[1,1]{1,0:T(1,128)}, bf16[128,4096]{1,0:T(8,128)(2,1)}, bf16[128,4096]{1,0:T(8,128)(2,1)}, f32[64,4096]{1,0:T(8,128)}, f32[64,1024]{1,0:T(8,128)}) custom-call(f32[1,1]{1,0:T(1,128)} %get-tuple-element.14.loss_in, bf16[128,4096]{1,0:T(8,128)(2,1)} %get-tuple-element.15.g1_in, bf16[128,4096]{1,0:T(8,128)(2,1)} %get-tuple-element.16.g2_in, ...), custom_call_target="tpu_custom_call" | custom-call | tf_op jit(solution)/shard_map/pallas_call | solution.py:529

commit v5 on v4

--- a/solution.py
+++ b/solution.py
@@ -22,8 +22,21 @@
 SLOT = {mask: slot for slot, mask in enumerate(ORDER)}
 BACK = {(7, 0): 1, (7, 1): 4}
 BACK.update({(mask, half): link for mask, link in ((6, 2), (3, 1), (5, 4), (1, 1), (2, 2), (4, 4)) for half in (0, 1)})
+AFTER = {(6, 0): 7, (3, 1): 7}
+AFTER.update({(mask, half): add for mask, add in ((1, 5), (2, 3), (4, 6)) for half in (0, 1)})
+STEPS = (
+    "Wc", "W7", "Q7", "K7", "k71", "k70", "K5", "q71", "Wr", "q70", "k50", "Q3", "k51", "Q6", "Q5", "K6", "k61",
+    "q30", "q61", "K3", "k30", "q50", "Q2", "k31", "Q4", "q60", "q31", "k60", "q51", "Q1", "K1", "K2", "K4", "q41",
+    "k10", "q20", "k20", "q10", "k41", "k11", "q40", "k40", "q21", "k21", "q11", "K0", "Q0",
+)
+SPANS = {"low": (0, 64), "high": (64, 128), "mid": (32, 96), "bottom": (0, 32), "top": (96, 128)}
+SPANS.update({"first": (0, 48), "second": (48, 80), "third": (80, 128)})
+TURNS = {4: (("low",), ("high",)), 2: (("high",), ("low",)), 1: (("mid",), ("bottom", "top"))}
+NEXT = {4: 2, 2: 1, 1: 4}
+CORNER = ((6, 4, "first", 1), (3, 2, "third", 4), (5, 1, "second", 2))
 HALF = ROWS // 2
-COPIES = 176
+SENDS, ARRIVALS = 14, 98
+OF_QUERIES, OF_KEYS, TO_CORE, OF_ROWS, OF_COLS, ROW_SWAP, CORE, PLANE, LOSS_PLANE, COLUMN, LOSS_COLUMN, PLANE_BACK, CORE_BACK, LOSS_SWAP = range(SENDS)
 TOTAL = MODEL + WIDTH
 HALF_RANK = RANK // 2
 PIECE = TOTAL // 8
@@ -42,33 +55,33 @@
 
 
 class Links:
-    def __init__(self, send_sems, recv_sems):
-        self.send_sems, self.recv_sems, self.count, self.sent = send_sems, recv_sems, 0, []
-
-    def copy(self, src, dst, device):
-        index = self.count
+    def __init__(self, send_sems, recv_sems, device):
+        self.send_sems, self.recv_sems, self.device, self.count = send_sems, recv_sems, device, 0
+
+    def slot(self):
         self.count += 1
-        made = pltpu.make_async_remote_copy(
+        return self.count - 1
+
+    def make(self, src, dst, device, batch, slot):
+        return pltpu.make_async_remote_copy(
             src_ref=src,
             dst_ref=dst,
-            send_sem=self.send_sems.at[index],
-            recv_sem=self.recv_sems.at[index],
+            send_sem=self.send_sems.at[batch],
+            recv_sem=self.recv_sems.at[slot],
             device_id=device,
             device_id_type=MESH,
         )
+
+    def copy(self, src, dst, device, batch, slot=None):
+        made = self.make(src, dst, device, batch, self.slot() if slot is None else slot)
         made.start()
-        self.sent.append(made)
         return made
 
-    def settle(self, made):
-        made.wait_recv()
-        made.wait_send()
-        self.sent = [copy for copy in self.sent if copy is not made]
-
-    def drain(self):
-        for made in self.sent:
-            made.wait_send()
-        self.sent = []
+    def sent(self, batch, whole):
+        self.make(whole, whole, self.device, batch, 0).wait_send()
+
+    def arrived(self, slot, whole):
+        self.make(whole, whole, self.device, 0, slot).wait_recv()
 
 
 def half_rows(half):
@@ -76,30 +89,31 @@
 
 
 class Group:
-    def __init__(self, links, near, data, stride, out, landing, part):
-        self.links, self.near, self.data, self.stride = links, near, data, stride
+    def __init__(self, links, near, data, stride, out, landing, part, ready, batch):
+        self.links, self.near, self.data, self.stride, self.ready, self.batch = links, near, data, stride, ready, batch
         self.out, self.landing, self.part, self.got, self.back_got = out, landing, part, {}, {}
 
-    def at(self, mask, half):
-        first = SLOT[mask] * self.stride + half * HALF
-        return self.data.at[first : first + HALF]
-
-    def give(self, mask, half, link):
+    def at(self, mask, part):
+        first, last = SPANS[part]
+        return self.data.at[SLOT[mask] * self.stride + first : SLOT[mask] * self.stride + last]
+
+    def give(self, mask, part, link):
         there = mask ^ link
-        self.got[there, half] = self.links.copy(self.at(mask, half), self.at(there, half), self.near[link])
-
-    def have(self, mask, half):
-        self.got[mask, half].wait_recv()
-
-    def back(self, mask, half, add=None):
-        rows = half_rows(half)
-        value = self.part(mask, rows)
+        self.got[there, part] = self.links.copy(self.at(mask, part), self.at(there, part), self.near[link], self.batch)
+
+    def have(self, mask, part):
+        self.got[mask, part].wait_recv()
+
+    def back(self, mask, half):
+        rows, add = half_rows(half), AFTER.get((mask, half))
         if add is not None:
             self.back_got[add, half].wait_recv()
-            value = value + self.landing[add - 1, rows].astype(F32)
-        self.out[mask - 1, rows] = value.astype(BF16)
+            value = self.part(mask, rows) + self.landing[add - 1, rows].astype(F32)
+            self.out[mask - 1, rows] = value.astype(BF16)
+        elif not self.ready:
+            self.out[mask - 1, rows] = self.part(mask, rows).astype(BF16)
         self.back_got[mask, half] = self.links.copy(
-            self.out.at[mask - 1, rows], self.landing.at[mask - 1, rows], self.near[BACK[mask, half]]
+            self.out.at[mask - 1, rows], self.landing.at[mask - 1, rows], self.near[BACK[mask, half]], self.batch
         )
 
     def whole(self):
@@ -140,15 +154,16 @@
 
     sibling = at(other=True)
     q_near, k_near = cube(False), cube(True)
-    plane = {(dx, dy): at(dx, dy) for dx in range(4) for dy in range(4) if dx or dy}
+    far_first = sorted(((dx, dy) for dx in range(4) for dy in range(4) if dx or dy), key=lambda d: -sum(min(c, 4 - c) for c in d))
+    plane = {step: at(*step) for step in far_first}
     column = {dz: at(dz=dz) for dz in (1, 2, 3)}
-    links = Links(send_sems, recv_sems)
+    links = Links(send_sems, recv_sems, sibling)
 
     loads = [
+        pltpu.make_async_copy(down_hbm, down, load_sems.at[2]),
         pltpu.make_async_copy(h1_hbm, h.at[0:ROWS], load_sems.at[0]),
+        pltpu.make_async_copy(up_hbm, up_ref, load_sems.at[3]),
         pltpu.make_async_copy(h2_hbm, h.at[ROWS : 2 * ROWS], load_sems.at[1]),
-        pltpu.make_async_copy(down_hbm, down, load_sems.at[2]),
-        pltpu.make_async_copy(up_hbm, up_ref, load_sems.at[3]),
         pltpu.make_async_copy(partner_hbm, partner_ref, load_sems.at[4]),
     ]
     for load in loads:
@@ -159,12 +174,12 @@
         pl.semaphore_signal(barrier, inc=1, device_id=device, device_id_type=MESH)
     rowacc[...] = jnp.zeros_like(rowacc)
     colacc[...] = jnp.zeros_like(colacc)
-    for load in loads:
-        load.wait()
-
-    low[...] = nt(h[...], down[...]).astype(BF16)
+
     for view, own in enumerate((q, k)):
         here = slice(view * ROWS, (view + 1) * ROWS)
+        for load in loads[3 * view : 3 * view + 3]:
+            load.wait()
+        low[here, :] = nt(h[here, :], down[...]).astype(BF16)
         mixed = h[here, 0:WIDTH].astype(F32) + nn(low[here, :], up_ref[...])
         inverse = lax.rsqrt(jnp.sum(mixed * mixed, axis=1, keepdims=True) + EPS)
         inv[here, :] = jnp.broadcast_to(inverse, (ROWS, LANES))
@@ -182,28 +197,35 @@
         first = SLOT[mask] * ROWS
         return pk[first + here.start : first + here.stop, :]
 
-    queries = Group(links, q_near, q, 2 * ROWS, q_out, q_in, q_part)
-    keys = Group(links, k_near, k, ROWS, k_out, k_in, k_part)
+    queries = Group(links, q_near, q, 2 * ROWS, q_out, q_in, q_part, False, OF_QUERIES)
+    keys = Group(links, k_near, k, ROWS, k_out, k_in, k_part, True, OF_KEYS)
     groups = (queries, keys)
 
-    def to_sibling(mask):
-        first = SLOT[mask] * 2 * ROWS
-        return links.copy(q.at[first : first + ROWS], q.at[first + ROWS : first + 2 * ROWS], sibling)
-
-    FIRST = {1: 0, 2: 1, 4: 0}
-    NEXT = {4: 2, 2: 1, 1: 4}
+    BATCH = {0: 0, 1: 0, 2: 0, 4: 0, 3: 1, 6: 1, 5: 1, 7: 2}
+    core_slots = [links.slot() for _ in range(3)]
+
+    def to_sibling(mask, first, last):
+        top = SLOT[mask] * 2 * ROWS
+        here, there = q.at[top + first : top + last], q.at[top + ROWS + first : top + ROWS + last]
+        links.copy(here, there, sibling, TO_CORE, core_slots[BATCH[mask]])
+
+    def sibling_has(batch, shards_of):
+        links.arrived(core_slots[batch], q.at[0 : shards_of * ROWS])
+
     for turn in (0, 1):
         for group in groups:
-            for link in (1, 2, 4):
-                group.give(0, FIRST[link] ^ turn, link)
-    passed = {0: to_sibling(0)}
+            for link in (4, 2, 1):
+                for part in TURNS[link][turn]:
+                    group.give(0, part, link)
+    to_sibling(0, 0, ROWS)
     for turn in (0, 1):
         for group in groups:
             for mask in (4, 2, 1):
-                group.have(mask, FIRST[mask] ^ turn)
-                group.give(mask, FIRST[mask] ^ turn, NEXT[mask])
-    for mask in (1, 2, 4):
-        passed[mask] = to_sibling(mask)
+                for part in TURNS[mask][turn]:
+                    group.have(mask, part)
+                    group.give(mask, part, NEXT[mask])
+                    if group is queries:
+                        to_sibling(mask, *SPANS[part])
 
     def score(first_row, row_count, first_col, col_count):
         columns = slice(first_col, first_col + col_count)
@@ -217,55 +239,59 @@
                 total = total + value[:, lane : lane + LANES]
             rowacc[here, :] += total
 
-    for mask in (0, 1, 2, 4):
-        passed[mask].wait_recv()
+    sibling_has(0, 4)
     score(0, 1024, 0, 512)
-    for group in groups:
-        group.have(6, 0)
-        group.give(6, 0, 1)
-        group.have(3, 1)
-        group.give(3, 1, 4)
-    for mask, half in ((6, 1), (3, 0), (5, 0), (5, 1)):
+    for turn in (0, 1):
         for group in groups:
-            group.have(mask, half)
-    for mask in (3, 6, 5):
-        passed[mask] = to_sibling(mask)
+            for mask, kind, corner, link in CORNER:
+                for part in TURNS[kind][turn]:
+                    group.have(mask, part)
+                    if group is queries:
+                        to_sibling(mask, *SPANS[part])
+                if turn == 0:
+                    group.give(mask, corner, link)
     score(0, 1024, 512, 256)
-    for mask in (3, 6, 5):
-        passed[mask].wait_recv()
+    sibling_has(1, 3)
     score(1024, 768, 0, 768)
-    for half in (0, 1):
-        queries.have(7, half)
-    passed[7] = to_sibling(7)
-    for half in (0, 1):
-        keys.have(7, half)
+    for corner in ("first", "second", "third"):
+        queries.have(7, corner)
+        to_sibling(7, *SPANS[corner])
+    for corner in ("first", "second", "third"):
+        keys.have(7, corner)
     score(0, 1792, 768, 256)
-    passed[7].wait_recv()
+    sibling_has(2, 1)
     score(1792, 256, 0, 1024)
-    links.drain()
+    links.sent(OF_QUERIES, q.at[0 : 7 * ROWS])
+    links.sent(OF_KEYS, k.at[0 : 7 * ROWS])
+    links.sent(TO_CORE, q.at[0 : 8 * ROWS])
+
 
     for block in range(8):
         cols[block : block + 1, :] = jnp.sum(colacc[:, block * LANES : (block + 1) * LANES], axis=0, keepdims=True)
-    col_copies = {m: links.copy(cols, col_in.at[m - 1], k_near[m]) for m in range(1, 8)}
+    col_slot = links.slot()
+    for m in (7, 6, 5, 3, 4, 2, 1):
+        links.copy(cols, col_in.at[m - 1], k_near[m], OF_COLS, col_slot)
     for block in range(16):
         lanes = rowacc[block * ROWS : (block + 1) * ROWS, :].T
         rows[block : block + 1, :] = jnp.sum(lanes, axis=0, keepdims=True)
-    row_swap = links.copy(rows, row_sib_in, sibling)
-    links.settle(row_swap)
+    row_swap = links.copy(rows, row_sib_in, sibling, ROW_SWAP)
+    row_swap.wait()
     for slot in range(8):
         for rank in range(2):
             here, there = slot * 2 + rank, slot * 2 + 1 - rank
             rows[here : here + 1, :] = rows[here : here + 1, :] + row_sib_in[there : there + 1, :]
-    row_copies = {m: links.copy(rows, row_in.at[m - 1], q_near[m]) for m in range(1, 8)}
+    row_slot = links.slot()
+    for m in (7, 6, 5, 3, 4, 2, 1):
+        links.copy(rows, row_in.at[m - 1], q_near[m], OF_ROWS, row_slot)
 
     choice = (lax.broadcasted_iota(jnp.int32, (ROWS, ROWS), 0) == partner_ref[...]).astype(BF16)
     pos[0:ROWS, :] = tn(choice, k[0:ROWS, :])
     pos[ROWS : 2 * ROWS, :] = nn(choice, q[0:ROWS, :])
     positive = SCALE * jnp.sum(q[0:ROWS, :].astype(F32) * pos[0:ROWS, :])
 
-    def cube_sum(total, arrived, copies, width):
-        for copy in copies.values():
-            links.settle(copy)
+    def cube_sum(total, arrived, batch, slot, width):
+        links.arrived(slot, arrived)
+        links.sent(batch, arrived)
         sums = []
         for mask in ORDER:
             value = total[SLOT[mask] * width : (SLOT[mask] + 1) * width, :]
@@ -275,27 +301,35 @@
             sums.append(value)
         return sums
 
-    sums_of_cols = cube_sum(cols, col_in, col_copies, 1)
+    sums_of_cols = cube_sum(cols, col_in, OF_COLS, col_slot, 1)
     for slot, value in enumerate(sums_of_cols):
         colb[0:1, slot * LANES : (slot + 1) * LANES] = 0.5 / value
-    sums_of_rows = cube_sum(rows, row_in, row_copies, 2)
+    sums_of_rows = cube_sum(rows, row_in, OF_ROWS, row_slot, 2)
     for slot, value in enumerate(sums_of_rows):
         rows[2 * slot : 2 * slot + 2, :] = 0.5 / value
 
-    def weigh(step, carry):
-        for part in range(2):
-            block = step * 2 + part
-            here = pl.ds(pl.multiple_of(block * ROWS, ROWS), ROWS)
-            row = jnp.broadcast_to(rows[pl.ds(block, 1), :], (ROWS, ROWS)).T
-            for lane in range(0, WIDTH, LANES):
-                columns = slice(lane, lane + LANES)
-                w[here, columns] = (expo[here, columns] * (row + colb[0:1, columns])).astype(BF16)
-        return carry
-
-    lax.fori_loop(0, 8, weigh, 0)
-
-    def key_part(first):
-        pk[first : first + 256, :] = tn(w[:, first : first + 256], q[...])
+    def weigh(first_block, count, first_lane, last_lane):
+        def blocks(step, carry):
+            for part in range(2):
+                block = first_block + step * 2 + part
+                here = pl.ds(pl.multiple_of(block * ROWS, ROWS), ROWS)
+                row = jnp.broadcast_to(rows[pl.ds(block, 1), :], (ROWS, ROWS)).T
+                for lane in range(first_lane, last_lane, LANES):
+                    columns = slice(lane, lane + LANES)
+                    w[here, columns] = (expo[here, columns] * (row + colb[0:1, columns])).astype(BF16)
+            return carry
+
+        lax.fori_loop(0, count // 2, blocks, 0)
+
+    def key_part(mask):
+        first = SLOT[mask] * ROWS
+        value = tn(w[:, first : first + ROWS], q[...])
+        for half in (0, 1):
+            here = half_rows(half)
+            if mask and (mask, half) not in AFTER:
+                k_out[mask - 1, here, :] = value[here].astype(BF16)
+            else:
+                pk[first + here.start : first + here.stop, :] = value[here]
 
     def query_part(mask):
         slot = SLOT[mask]
@@ -303,46 +337,32 @@
         part = nn(w[here : here + 2 * ROWS, :], k[...])
         pq[slot, :, :] = part[0:ROWS]
         sib_out[slot, :, :] = part[ROWS:].astype(BF16)
-        sib[mask] = links.copy(sib_out.at[slot], sib_in.at[slot], sibling)
-
-    query_part(7)
-    key_part(768)
-    for mask, half in ((7, 0), (7, 1), (5, 0), (5, 1)):
-        keys.back(mask, half)
-    sib[7].wait_recv()
-    queries.back(7, 0)
-    queries.back(7, 1)
-    for mask in (5, 3, 6):
-        query_part(mask)
-    key_part(512)
-    keys.back(3, 0)
-    keys.back(6, 1)
-    sib[5].wait_recv()
-    queries.back(5, 0)
-    queries.back(5, 1)
-    sib[3].wait_recv()
-    queries.back(3, 0)
-    sib[6].wait_recv()
-    queries.back(6, 1)
-
-    key_part(256)
-    keys.back(6, 0, 7)
-    keys.back(3, 1, 7)
-    queries.back(6, 0, 7)
-    queries.back(3, 1, 7)
-    for mask in (1, 2, 4):
-        query_part(mask)
-    key_part(0)
-    for mask in (1, 2, 4):
-        sib[mask].wait_recv()
-    for mask, half, add in ((1, 0, 5), (2, 0, 3), (4, 1, 6), (1, 1, 5), (4, 0, 6), (2, 1, 3)):
-        for group in groups:
-            group.back(mask, half, add)
-    query_part(0)
+        sib[mask] = links.copy(sib_out.at[slot], sib_in.at[slot], sibling, TO_CORE)
+
+    waited = set()
+    for step in STEPS:
+        kind, mask = step[0], step[1]
+        if step == "W7":
+            weigh(14, 2, 0, WIDTH)
+        elif step == "Wc":
+            weigh(0, 14, 6 * LANES, WIDTH)
+        elif step == "Wr":
+            weigh(0, 14, 0, 6 * LANES)
+        elif kind == "Q":
+            query_part(int(mask))
+        elif kind == "K":
+            key_part(int(mask))
+        elif kind == "k":
+            keys.back(int(mask), int(step[2]))
+        else:
+            if mask not in waited:
+                waited.add(mask)
+                sib[int(mask)].wait_recv()
+            queries.back(int(mask), int(step[2]))
 
     terms = 0.5 * jnp.sum(jnp.log(sums_of_rows[0][0:1, :])) + 0.5 * jnp.sum(jnp.log(sums_of_cols[0])) - positive
     loss_core[core, :, :] = jnp.broadcast_to(terms, (8, LANES))
-    loss_swap = links.copy(loss_core.at[core], loss_core.at[core], sibling)
+    loss_swap = links.copy(loss_core.at[core], loss_core.at[core], sibling, LOSS_SWAP)
     loss_swap.wait_recv()
     loss_plane[place, :, :] = jnp.sum(loss_core[...], axis=0)
     sib[0].wait_recv()
@@ -366,7 +386,7 @@
 
     mine = pl.ds(pl.multiple_of(core * HALF_RANK, HALF_RANK), HALF_RANK)
     theirs = pl.ds(pl.multiple_of((1 - core) * HALF_RANK, HALF_RANK), HALF_RANK)
-    core_got = links.copy(gsend.at[theirs], core_in, sibling)
+    core_got = links.copy(gsend.at[theirs], core_in, sibling, CORE)
     core_got.wait_recv()
     for piece in range(16):
         top, side = (piece // 8) * 16, (piece % 8) * PIECE
@@ -374,12 +394,11 @@
         value = gsum[pl.ds(pl.multiple_of(core * HALF_RANK + top, 16), 16), columns]
         value = value + core_in[top : top + 16, columns].astype(F32)
         plane_out[piece, :, :] = value.astype(BF16)
-    plane_got = []
+    plane_slot, loss_slot = links.slot(), links.slot()
     for (dx, dy), device in plane.items():
         there = lax.rem(x + dx, 4) * 4 + lax.rem(y + dy, 4)
-        plane_got.append(links.copy(plane_out.at[there], plane_in.at[place], device))
+        links.copy(plane_out.at[there], plane_in.at[place], device, PLANE, plane_slot)
     plane_in[place, :, :] = plane_out[place]
-    loss_got = [links.copy(loss_plane.at[place], loss_plane.at[place], device) for device in plane.values()]
     stores = []
     for view, target in enumerate((g1_hbm, g2_hbm)):
         here = slice(view * ROWS, (view + 1) * ROWS)
@@ -393,33 +412,49 @@
         lax.fori_loop(0, (MODEL - WIDTH) // 512, chunk, 0)
         stores.append(pltpu.make_async_copy(state.at[view], target, load_sems.at[view]))
         stores[-1].start()
-    for copy in plane_got:
-        copy.wait_recv()
+    for device in plane.values():
+        links.copy(loss_plane.at[place], loss_plane.at[place], device, LOSS_PLANE, loss_slot)
+    links.arrived(plane_slot, plane_in.at[0:15])
     z_all[z, :, :] = jnp.sum(plane_in[...].astype(F32), axis=0).astype(BF16)
-    z_got = [links.copy(z_all.at[z], z_all.at[z], device) for device in column.values()]
-    for copy in loss_got:
-        copy.wait_recv()
+    z_slot, loss_z_slot = links.slot(), links.slot()
+    for device in column.values():
+        links.copy(z_all.at[z], z_all.at[z], device, COLUMN, z_slot)
+    links.arrived(loss_slot, loss_plane.at[0:15])
     loss_z[z, :, :] = jnp.sum(loss_plane[...], axis=0)
-    loss_got = [links.copy(loss_z.at[z], loss_z.at[z], device) for device in column.values()]
-    for copy in z_got:
-        copy.wait_recv()
+    for device in column.values():
+        links.copy(loss_z.at[z], loss_z.at[z], device, LOSS_COLUMN, loss_z_slot)
+    links.arrived(z_slot, z_all.at[0:3])
     sums[place, :, :] = jnp.sum(z_all[...].astype(F32), axis=0).astype(BF16)
-    plane_back = {step: links.copy(sums.at[place], sums.at[place], device) for step, device in plane.items()}
-    core_back = [links.copy(sums.at[place], sums_hbm.at[core, place], sibling)]
-    for copy in loss_got:
-        copy.wait_recv()
+    plane_back = {
+        step: links.copy(sums.at[place], sums.at[place], device, PLANE_BACK) for step, device in plane.items()
+    }
+    core_slot = links.slot()
+    links.copy(sums.at[place], sums_hbm.at[core, place], sibling, CORE_BACK, core_slot)
+    links.arrived(loss_z_slot, loss_z.at[0:3])
     loss_ref[0, 0] = jnp.sum(jnp.sum(loss_z[...], axis=0)[0:1, 0:1]) * (1.0 / TEXTS) + SCALE
     for (dx, dy), copy in plane_back.items():
         copy.wait_recv()
         came = lax.rem(x + 4 - dx, 4) * 4 + lax.rem(y + 4 - dy, 4)
-        core_back.append(links.copy(sums.at[came], sums_hbm.at[core, came], sibling))
+        links.copy(sums.at[came], sums_hbm.at[core, came], sibling, CORE_BACK, core_slot)
     stores.append(pltpu.make_async_copy(sums, sums_hbm.at[core], load_sems.at[2]))
     stores[-1].start()
-    for copy in core_back:
-        copy.wait_recv()
+    links.sent(OF_QUERIES, q_out)
+    links.sent(OF_KEYS, k_out)
+    links.sent(TO_CORE, sib_out)
+    for batch, whole in (
+        (LOSS_SWAP, loss_core.at[0]),
+        (CORE, core_in),
+        (PLANE, plane_in.at[0:15]),
+        (LOSS_PLANE, loss_plane.at[0:15]),
+        (COLUMN, z_all.at[0:3]),
+        (LOSS_COLUMN, loss_z.at[0:3]),
+        (PLANE_BACK, sums.at[0:15]),
+        (CORE_BACK, sums),
+    ):
+        links.sent(batch, whole)
+    links.arrived(core_slot, sums)
     for store in stores:
         store.wait()
-    links.drain()
 
 
 def finish(
@@ -519,8 +554,8 @@
             pltpu.VMEM((16, 8, LANES), F32),
             pltpu.VMEM((4, 8, LANES), F32),
             pltpu.SemaphoreType.DMA((5,)),
-            pltpu.SemaphoreType.DMA((COPIES,)),
-            pltpu.SemaphoreType.DMA((COPIES,)),
+            pltpu.SemaphoreType.DMA((SENDS,)),
+            pltpu.SemaphoreType.DMA((ARRIVALS,)),
         ],
         compiler_params=pltpu.CompilerParams(
             collective_id=0, has_side_effects=True, vmem_limit_bytes=60 * 1024 * 1024

time: 87.9 us -> 83.5 us (0.950)
  Pallas kernels: 86.9 us -> 82.5 us
    pallas_call x1, Pallas kernels: 82.6 us -> 78.2 us  [shards(): pl.pallas_call(body, out_shape=(jax.ShapeDtypeStruct((1, 1), F32), jax.Sh...]
where the time goes in v5:
time: 83.5 us; the launch traced here: 83.3 us
  Pallas kernels  82.5 us (99%)
    pallas_call x1, Pallas kernels, shards(): pl.pallas_call(body, out_shape=(jax.ShapeDtypeStruct((1, 1), F32), jax.Sh...  78.2 us
    pallas_call x1, Pallas kernels, shards(): pl.pallas_call(finish, out_shape=(jax.ShapeDtypeStruct((1, 1), F32), jax....  4.24 us

profile of v5, /device:TPU:1, one launch (start us, length us, event | category | flops | bytes accessed | tf_op | source)
XLA Modules:
  0.0 83.3 jit_solution(2457513731303911714)
XLA Ops:
  0.6 78.2 %shard_map.92 = (f32[1,1]{1,0:T(1,128)}, bf16[128,4096]{1,0:T(8,128)(2,1)}, bf16[128,4096]{1,0:T(8,128)(2,1)}, bf16[2,16,16,640]{3,2,1,0:T(8,128)(2,1)}) custom-call(bf16[128,4096]{1,0:T(8,128)(2,1)} %h1_hbm.1, bf16[128,4096]{1,0:T(8,128)(2,1)} %h2_hbm.1, s32[1,128]{1,0:T(1,128)} %partner_hbm.1, bf16[64,4096]{1,0:T(8,128)(2,1)} %bitcast.3, ...), custom_call_target="tpu_custom_call" | custom-call | tf_op jit(solution)/shard_map/pallas_call | solution.py:504
  78.9 4.2 %shard_map.93 = (f32[1,1]{1,0:T(1,128)}, bf16[128,4096]{1,0:T(8,128)(2,1)}, bf16[128,4096]{1,0:T(8,128)(2,1)}, f32[64,4096]{1,0:T(8,128)}, f32[64,1024]{1,0:T(8,128)}) custom-call(f32[1,1]{1,0:T(1,128)} %get-tuple-element.14.loss_in, bf16[128,4096]{1,0:T(8,128)(2,1)} %get-tuple-element.15.g1_in, bf16[128,4096]{1,0:T(8,128)(2,1)} %get-tuple-element.16.g2_in, ...), custom_call_target="tpu_custom_call" | custom-call | tf_op jit(solution)/shard_map/pallas_call | solution.py:564

commit v6 on v5

--- a/solution.py
+++ b/solution.py
@@ -25,9 +25,9 @@
 AFTER = {(6, 0): 7, (3, 1): 7}
 AFTER.update({(mask, half): add for mask, add in ((1, 5), (2, 3), (4, 6)) for half in (0, 1)})
 STEPS = (
-    "Wc", "W7", "Q7", "K7", "k71", "k70", "K5", "q71", "Wr", "q70", "k50", "Q3", "k51", "Q6", "Q5", "K6", "k61",
-    "q30", "q61", "K3", "k30", "q50", "Q2", "k31", "Q4", "q60", "q31", "k60", "q51", "Q1", "K1", "K2", "K4", "q41",
-    "k10", "q20", "k20", "q10", "k41", "k11", "q40", "k40", "q21", "k21", "q11", "K0", "Q0",
+    "W7", "Q7", "Wc", "Wr", "Q5", "q70", "q71", "K7", "k71", "k70", "Q3", "Q6", "K6", "k61", "q51", "K3", "q30",
+    "k30", "K5", "k51", "K0", "q60", "q50", "q61", "K4", "q31", "k31", "k60", "k50", "Q2", "Q1", "Q4", "K2", "k41",
+    "K1", "k20", "q11", "q20", "k11", "q40", "q21", "k10", "q10", "k40", "k21", "q41", "Q0",
 )
 SPANS = {"low": (0, 64), "high": (64, 128), "mid": (32, 96), "bottom": (0, 32), "top": (96, 128)}
 SPANS.update({"first": (0, 48), "second": (48, 80), "third": (80, 128)})
@@ -306,14 +306,17 @@
         colb[0:1, slot * LANES : (slot + 1) * LANES] = 0.5 / value
     sums_of_rows = cube_sum(rows, row_in, OF_ROWS, row_slot, 2)
     for slot, value in enumerate(sums_of_rows):
-        rows[2 * slot : 2 * slot + 2, :] = 0.5 / value
+        half = 0.5 / value
+        for rank in range(2):
+            first = (2 * slot + rank) * ROWS
+            rowacc[first : first + ROWS, :] = jnp.broadcast_to(half[rank : rank + 1, :], (ROWS, LANES)).T
 
     def weigh(first_block, count, first_lane, last_lane):
         def blocks(step, carry):
             for part in range(2):
                 block = first_block + step * 2 + part
                 here = pl.ds(pl.multiple_of(block * ROWS, ROWS), ROWS)
-                row = jnp.broadcast_to(rows[pl.ds(block, 1), :], (ROWS, ROWS)).T
+                row = rowacc[here, :]
                 for lane in range(first_lane, last_lane, LANES):
                     columns = slice(lane, lane + LANES)
                     w[here, columns] = (expo[here, columns] * (row + colb[0:1, columns])).astype(BF16)

time: 83.5 us -> 81.4 us (0.975)
  Pallas kernels: 82.5 us -> 80.4 us
    pallas_call x1, Pallas kernels: 78.2 us -> 76.2 us  [shards(): pl.pallas_call(body, out_shape=(jax.ShapeDtypeStruct((1, 1), F32), jax.Sh...]
where the time goes in v6:
time: 81.4 us; the launch traced here: 81.2 us
  Pallas kernels  80.4 us (99%)
    pallas_call x1, Pallas kernels, shards(): pl.pallas_call(body, out_shape=(jax.ShapeDtypeStruct((1, 1), F32), jax.Sh...  76.2 us
    pallas_call x1, Pallas kernels, shards(): pl.pallas_call(finish, out_shape=(jax.ShapeDtypeStruct((1, 1), F32), jax....  4.24 us

profile of v6, /device:TPU:1, one launch (start us, length us, event | category | flops | bytes accessed | tf_op | source)
XLA Modules:
  0.0 81.2 jit_solution(9707365657140013319)
XLA Ops:
  0.6 76.2 %shard_map.92 = (f32[1,1]{1,0:T(1,128)}, bf16[128,4096]{1,0:T(8,128)(2,1)}, bf16[128,4096]{1,0:T(8,128)(2,1)}, bf16[2,16,16,640]{3,2,1,0:T(8,128)(2,1)}) custom-call(bf16[128,4096]{1,0:T(8,128)(2,1)} %h1_hbm.1, bf16[128,4096]{1,0:T(8,128)(2,1)} %h2_hbm.1, s32[1,128]{1,0:T(1,128)} %partner_hbm.1, bf16[64,4096]{1,0:T(8,128)(2,1)} %bitcast.3, ...), custom_call_target="tpu_custom_call" | custom-call | tf_op jit(solution)/shard_map/pallas_call | solution.py:507
  76.8 4.2 %shard_map.93 = (f32[1,1]{1,0:T(1,128)}, bf16[128,4096]{1,0:T(8,128)(2,1)}, bf16[128,4096]{1,0:T(8,128)(2,1)}, f32[64,4096]{1,0:T(8,128)}, f32[64,1024]{1,0:T(8,128)}) custom-call(f32[1,1]{1,0:T(1,128)} %get-tuple-element.14.loss_in, bf16[128,4096]{1,0:T(8,128)(2,1)} %get-tuple-element.15.g1_in, bf16[128,4096]{1,0:T(8,128)(2,1)} %get-tuple-element.16.g2_in, ...), custom_call_target="tpu_custom_call" | custom-call | tf_op jit(solution)/shard_map/pallas_call | solution.py:567
